TPU v7x, 32 devices: a whole 2x2x4 slice. The times are simulated.
32 devices in a mesh: cohort: 4 (over x, core), person: 8 (over z, y).
Axes of the slice: x: 2, y: 2, z: 4, core: 2. Of those that a mesh axis runs over, the one named last changes fastest.
Arguments:
- dosages: bfloat16 [4, 1024, 1536], P('cohort', 'person'), may hold values from 0 to 2
- allele_counts: int32 [4, 8, 1536], P('cohort', 'person'), may hold values from 0 to 256, as said below
- partner: int32 [4], replicated, may hold values from 0 to 3, as said below
Outputs:
- relation: bfloat16 [4, 1024, 1024], P('cohort', 'person')
Inputs may be any that keep to these rules, and one draw needn't show every extreme that they name: `allele_counts`: each entry lies between 0 and 256, and some entry equals 256. partner[c] = c XOR r for one round number r with 1 <= r < 4, the same for every c.
All inputs are finite; a program needn't handle non-finite values.
Results may differ from a plain program's by a relative error of at most 0.0058.
Values may be sent and summed in bfloat16 or wider, within the bound.
No kernel may reach another device: no remote copies, remote signals or barrier semaphores. Data moves between devices by JAX's collectives and lax.ppermute only.
A program may use at most 64 MiB of HBM per device.

v0:
```python
import math

import jax
import jax.numpy as jnp
from jax import lax
from jax.sharding import PartitionSpec as P


def partner_2(shard, axis, stride):
    return lax.ppermute(shard, axis, [(i, i ^ 1 << stride) for i in range(lax.axis_size(axis))])


def cross_product(left_rows, right_rows, markers):
    product = lax.dot_general(
        left_rows, right_rows, (((1,), (1,)), ((), ())), preferred_element_type=jnp.float32
    )
    return (product / math.sqrt(markers)).astype(jnp.bfloat16)


def on_device(dosages, allele_counts, partner):
    local_rows = dosages[0]
    markers = local_rows.shape[1]
    people_dev = local_rows.shape[0]
    blocks = lax.axis_size("person")
    people_all = people_dev * blocks
    totals = lax.psum(allele_counts, "person")
    freq = (totals[0, 0].astype(jnp.float32) + 1.0) / (2.0 * people_all + 2.0)
    spread = jnp.sqrt(2.0 * freq * (1.0 - freq))
    standard = ((local_rows.astype(jnp.float32) - 2.0 * freq) / spread).astype(jnp.bfloat16)
    own_cohort = lax.axis_index("cohort")
    other_cohort = partner[own_cohort]
    round_number = jnp.bitwise_xor(other_cohort, own_cohort)
    bit_count = lax.axis_size("cohort").bit_length() - 1
    partner_rows = standard
    for bit_number in range(bit_count):
        moved = partner_2(partner_rows, "cohort", bit_number)
        flag = jnp.bitwise_and(jnp.right_shift(round_number, bit_number), 1) == 1
        partner_rows = jnp.where(flag, moved, partner_rows)
    relation = cross_product(
        standard, lax.all_gather(partner_rows, "person", axis=0, tiled=True), markers
    )
    return relation[None]


def solution(mesh):
    placed = (P("cohort", "person", None), P("cohort", "person", None), P())
    return jax.shard_map(
        on_device,
        mesh=mesh,
        in_specs=placed,
        out_specs=P("cohort", "person", None),
        check_vma=False,
    )
```

profile of v0, /device:TPU:1, one launch (start us, length us, event | category | flops | bytes accessed | tf_op | source)
XLA Modules:
  0.0 104.5 jit_solution(4545076060520222557)
XLA Ops:
  6.5 0.0 all-gather.2.cloned.1.call-start
  6.5 9.8 %psum.7 = s32[1,1,1536]{2,1,0:T(1,128)S(1)} all-reduce(s32[1,1,1536]{2,1,0:T(1,128)} %param.4), channel_id=1, replica_groups=mesh['cohort'=4,'person'=8] {'person'}, use_global_device_ids=true, to_apply=%region_0.0 | all-reduce | flops 1536 | bytes 12288 | tf_op jit(solution)/shard_map/psum | solution.py:26
  16.4 1.1 %fusion.3 = bf16[128,1536]{1,0:T(8,128)(2,1)S(1)} fusion(bf16[1,128,1536]{2,1,0:T(8,128)(2,1)} %param.3, f32[1536]{0:T(1024)S(1)} %multiply_sqrt_fusion, f32[1536]{0:T(1024)S(1)} %get-tuple-element.6), kind=kLoop, calls=%fused_computation.5 | loop fusion | flops 786432 | bytes 798720 | tf_op jit(solution)/shard_map/convert_element_type | solution.py:29
  17.5 3.6 %collective-permute-start = (bf16[128,1536]{1,0:T(8,128)(2,1)S(1)}, bf16[128,1536]{1,0:T(8,128)(2,1)S(1)}, u32[]{:S(2)}, u32[]{:S(2)}) collective-permute-start(bf16[128,1536]{1,0:T(8,128)(2,1)S(1)} %fusion.3), channel_id=1, source_target_pairs={{0,8},{8,0},{16,24},{24,16},{1,9},{9,1},{17,25},{25,17},{2,10},{10... | collective-permute-start | bytes 1179656 | tf_op jit(solution)/shard_map/ppermute | solution.py:10
  21.2 1.2 %dynamic_slice.3 = s32[1]{0:T(128)} dynamic-slice(s32[4]{0:T(128)} %param.5, s32[]{:T(128)S(6)} %select_n.17), dynamic_slice_sizes={1} | dynamic-slice | bytes 12 | tf_op jit(solution)/shard_map/dynamic_slice | solution.py:31
  23.0 0.0 collective-permute-done
  23.1 1.1 %broadcast_select_fusion = bf16[128,1536]{1,0:T(8,128)(2,1)S(1)} fusion(bf16[128,1536]{1,0:T(8,128)(2,1)S(1)} %collective-permute-done, pred[]{:T(512)S(6)} %eq.7, f32[1536]{0:T(1024)S(1)} %multiply_sqrt_fusion, f32[1536]{0:T(1024)S(1)} %get-tuple-element.6, bf16[1,128,1536]{2,1,0:T(8,128)(2,1)} %param.3), kind=kLoop, calls=%fused_computation.6 | loop fusion | flops 983040 | bytes 1191937 | tf_op jit(solution)/shard_map/jit(_where)/select_n | solution.py:38
  24.2 1.3 %collective-permute-start.1 = (bf16[128,1536]{1,0:T(8,128)(2,1)S(1)}, bf16[128,1536]{1,0:T(8,128)(2,1)S(1)}, u32[]{:S(2)}, u32[]{:S(2)}) collective-permute-start(bf16[128,1536]{1,0:T(8,128)(2,1)S(1)} %broadcast_select_fusion), channel_id=1, source_target_pairs={{0,16},{8,24},{16,0},{24,8},{1,17},{9,25},{17,1},{25,9},{2,18},{10... | collective-permute-start | bytes 1179656 | tf_op jit(solution)/shard_map/ppermute | solution.py:10
  25.5 9.5 %collective-permute-done.1 = bf16[128,1536]{1,0:T(8,128)(2,1)S(1)} collective-permute-done((bf16[128,1536]{1,0:T(8,128)(2,1)S(1)}, bf16[128,1536]{1,0:T(8,128)(2,1)S(1)}, u32[]{:S(2)}, u32[]{:S(2)}) %collective-permute-start.1) | collective-permute-done | bytes 393248 | tf_op jit(solution)/shard_map/ppermute | solution.py:10
  35.0 0.8 broadcast_select_fusion.1
  35.8 0.0 all-gather.2.cloned.1.call-update
  35.8 58.1 %all-gather.2.cloned.1.call-done = bf16[1024,1536]{1,0:T(8,128)(2,1)} async-done(((bf16[128,1536]{1,0:T(8,128)(2,1)}), bf16[1024,1536]{1,0:T(8,128)(2,1)}) %all-gather.2.cloned.1.call-update) | async-done | bytes 3145744 | tf_op jit(solution)/shard_map/all_gather | solution.py:40
  93.9 3.7 %fusion.1 = bf16[1,128,1024]{2,1,0:T(8,128)(2,1)} fusion(bf16[128,1536]{1,0:T(8,128)(2,1)S(1)} %fusion.3, bf16[1024,1536]{1,0:T(8,128)(2,1)} %all-gather.2.cloned.1.call-done), kind=kOutput, calls=%fused_computation.2 | convolution fusion | flops 402915328 | bytes 3801088 | tf_op jit(solution)/shard_map/dot_general | solution.py:14
  (2 shorter events, 0.0 us)
Async XLA Ops:
  6.5 87.4 %all-gather.2.cloned.1.call-start = ((), (), s32[]{:S(2)}) async-start(), calls=%async_computation | async-start | bytes 3538944 | tf_op jit(solution)/shard_map/all_gather | solution.py:40
  17.5 5.5 %collective-permute-start = (bf16[128,1536]{1,0:T(8,128)(2,1)S(1)}, bf16[128,1536]{1,0:T(8,128)(2,1)S(1)}, u32[]{:S(2)}, u32[]{:S(2)}) collective-permute-start(bf16[128,1536]{1,0:T(8,128)(2,1)S(1)} %fusion.3), channel_id=1, source_target_pairs={{0,8},{8,0},{16,24},{24,16},{1,9},{9,1},{17,25},{25,17},{2,10},{10... | collective-permute-start | bytes 1179656 | tf_op jit(solution)/shard_map/ppermute | solution.py:10
  24.2 10.8 %collective-permute-start.1 = (bf16[128,1536]{1,0:T(8,128)(2,1)S(1)}, bf16[128,1536]{1,0:T(8,128)(2,1)S(1)}, u32[]{:S(2)}, u32[]{:S(2)}) collective-permute-start(bf16[128,1536]{1,0:T(8,128)(2,1)S(1)} %broadcast_select_fusion), channel_id=1, source_target_pairs={{0,16},{8,24},{16,0},{24,8},{1,17},{9,25},{17,1},{25,9},{2,18},{10... | collective-permute-start | bytes 1179656 | tf_op jit(solution)/shard_map/ppermute | solution.py:10
Sparse Core Ops, SparseCore 0:
  35.9 57.9 all-gather.1
where the time goes:
time: 106 us; the launch traced here: 105 us
  waiting for transfers between devices  67.7 us (64%)
  between operations  14.1 us (13%)
  blocking collectives  9.83 us (9%)
  starting transfers between devices  4.91 us (5%)
  matrix products  3.73 us (4%)
  other arithmetic  3.08 us (3%)
  local copies, waits for them, and re-layouts  1.24 us (1%)
    all_gather x1, waiting for transfers between devices, on_device(): lax.all_gather(partner_rows, 'person', axis=0, tiled=True)  58.1 us
    psum x1, blocking collectives, on_device(): totals = lax.psum(allele_counts, 'person')  9.83 us
    ppermute x2, waiting for transfers between devices, partner_2(): lax.ppermute(shard, axis, [(i, i ^ 1 << stride) for i in range(lax.axis_s...  9.52 us
    ppermute x2, starting transfers between devices, partner_2(): lax.ppermute(shard, axis, [(i, i ^ 1 << stride) for i in range(lax.axis_s...  4.91 us
    dot_general x1, matrix products, cross_product(): lax.dot_general(left_rows, right_rows, (((1,), (1,)), ((), ())), preferre...  3.73 us
  transfers between devices with their start and end apart: 3, of which 2 were waited for; matrix products, arithmetic and copies ran while one was open for 1% of the time, Pallas kernels for 0%

commit v1 on v0

v1 whole, which is shorter than its diff:
```python
import functools
import math

import jax
import jax.numpy as jnp
from jax import lax
from jax.experimental import pallas as pl
from jax.experimental.pallas import tpu as pltpu
from jax.sharding import PartitionSpec as P

AXES = ("cohort", "person")
VMEM_BYTES = 48 * 1024 * 1024


def left_cohorts(cohorts, round_number):
    if round_number == 1:
        return [c for c in range(cohorts) if c & 1 == 0]
    top = 1 << (round_number.bit_length() - 1)
    return [
        c
        for c in range(cohorts)
        if (c & top == 0 and c & 1 == 0) or (c & top and (c ^ round_number ^ 1) & 1 == 0)
    ]


def group_size(blocks):
    return 1 << (blocks.bit_length() // 2)


def standard_rows(rows, totals, people_all):
    freq = (totals.astype(jnp.float32) + 1.0) / (2.0 * people_all + 2.0)
    scale = 1.0 / jnp.sqrt(2.0 * freq * (1.0 - freq))
    return ((rows.astype(jnp.float32) - 2.0 * freq) * scale).astype(jnp.bfloat16)


def tile_kernel(near, far, people_all, root, *refs):
    lefts, rights = refs[:near], refs[near : near + far]
    left_totals, right_totals, left_out, right_out, left_std, right_std = refs[near + far :]
    rows = lefts[0].shape[0]
    for m in range(far):
        right_std[m * rows : (m + 1) * rows, :] = standard_rows(
            rights[m][...], right_totals[...], people_all
        )
    for d in range(near):
        left_std[d * rows : (d + 1) * rows, :] = standard_rows(
            lefts[d][...], left_totals[...], people_all
        )
    contract = (((1,), (1,)), ((), ()))
    for d in range(near):
        product = lax.dot_general(
            left_std[d * rows : (d + 1) * rows, :],
            right_std[...],
            contract,
            preferred_element_type=jnp.float32,
        )
        left_out[d] = (product / root).astype(jnp.bfloat16)
    for m in range(far):
        product = lax.dot_general(
            right_std[m * rows : (m + 1) * rows, :],
            left_std[...],
            contract,
            preferred_element_type=jnp.float32,
        )
        right_out[m] = (product / root).astype(jnp.bfloat16)


def tile(lefts, rights, left_totals, right_totals, people_all):
    near, far = len(lefts), len(rights)
    rows, markers = lefts[0].shape
    return pl.pallas_call(
        functools.partial(tile_kernel, near, far, people_all, math.sqrt(markers)),
        out_shape=(
            jax.ShapeDtypeStruct((near, rows, far * rows), jnp.bfloat16),
            jax.ShapeDtypeStruct((far, rows, near * rows), jnp.bfloat16),
        ),
        scratch_shapes=[
            pltpu.VMEM((near * rows, markers), jnp.bfloat16),
            pltpu.VMEM((far * rows, markers), jnp.bfloat16),
        ],
        compiler_params=pltpu.CompilerParams(vmem_limit_bytes=VMEM_BYTES),
    )(*lefts, *rights, left_totals, right_totals)


def place_kernel(near, far, where_ref, *refs):
    left_parts, right_parts, out_ref = refs[:near], refs[near : near + far], refs[near + far]
    rows = out_ref.shape[1]
    place = where_ref[1]

    def columns(d, m):
        block = jnp.bitwise_xor(place, d + near * m)
        return pl.ds(pl.multiple_of(block * rows, rows), rows)

    @pl.when(where_ref[0] == 1)
    def _():
        for d in range(near):
            for m in range(far):
                out_ref[0, :, columns(d, m)] = left_parts[d][:, m * rows : (m + 1) * rows]

    @pl.when(where_ref[0] == 0)
    def _():
        for d in range(near):
            for m in range(far):
                out_ref[0, :, columns(d, m)] = right_parts[m][:, d * rows : (d + 1) * rows]


def place_blocks(is_left, place, left_parts, right_parts):
    near, far = len(left_parts), len(right_parts)
    rows = left_parts[0].shape[0]
    where = jnp.stack([is_left.astype(jnp.int32), place])
    vmem = pl.BlockSpec(memory_space=pltpu.VMEM)
    return pl.pallas_call(
        functools.partial(place_kernel, near, far),
        out_shape=jax.ShapeDtypeStruct((1, rows, near * far * rows), jnp.bfloat16),
        in_specs=[pl.BlockSpec(memory_space=pltpu.SMEM)] + [vmem] * (near + far),
        out_specs=vmem,
        compiler_params=pltpu.CompilerParams(vmem_limit_bytes=VMEM_BYTES),
    )(where, *left_parts, *right_parts)


def one_round(round_number, cohorts, blocks, dosages, allele_counts):
    own = dosages[0]
    people_all = own.shape[0] * blocks
    near = group_size(blocks)
    far = blocks // near
    left = left_cohorts(cohorts, round_number)

    def among_left(d):
        return [(c * blocks + i, c * blocks + (i ^ d)) for c in left for i in range(blocks)]

    def to_left(m):
        return [
            ((c ^ round_number) * blocks + (i ^ near * m), c * blocks + i)
            for c in left
            for i in range(blocks)
        ]

    def from_left(m):
        return [(b, a) for a, b in to_left(m)]

    lefts = [own] + [lax.ppermute(own, AXES, among_left(d)) for d in range(1, near)]
    rights = [lax.ppermute(own, AXES, to_left(m)) for m in range(far)]
    totals = lax.psum(allele_counts[0], "person")
    right_totals = lax.ppermute(totals, AXES, to_left(0))
    left_out, right_out = tile(lefts, rights, totals, right_totals, people_all)
    left_parts = [left_out[0]] + [
        lax.ppermute(left_out[d], AXES, among_left(d)) for d in range(1, near)
    ]
    right_parts = [lax.ppermute(right_out[m], AXES, from_left(m)) for m in range(far)]
    cohort = lax.axis_index("cohort")
    is_left = functools.reduce(jnp.logical_or, [cohort == c for c in left])
    return place_blocks(is_left, lax.axis_index("person"), left_parts, right_parts)


def on_device(dosages, allele_counts, partner):
    cohorts, blocks = lax.axis_size("cohort"), lax.axis_size("person")
    rounds = [
        functools.partial(one_round, round_number, cohorts, blocks)
        for round_number in range(1, cohorts)
    ]
    return lax.switch(partner[0] - 1, rounds, dosages, allele_counts)


def solution(mesh):
    placed = (P("cohort", "person", None), P("cohort", "person", None), P())
    return jax.shard_map(
        on_device,
        mesh=mesh,
        in_specs=placed,
        out_specs=P("cohort", "person", None),
        check_vma=False,
    )
```

time: 106 us -> 61.1 us (0.58)
  the two profiles are of different devices: /device:TPU:1 before, /device:TPU:0 now
where the time goes in v1:
time: 61.1 us; the launch traced here: 60.6 us
  starting transfers between devices  24.9 us (41%)
  waiting for transfers between devices  17 us (28%)
  blocking collectives  13.2 us (22%)
  Pallas kernels  3.76 us (6%)
  local copies, waits for them, and re-layouts  1.4 us (2%)
    psum x1, blocking collectives, one_round(): totals = lax.psum(allele_counts[0], 'person')  13.2 us
    ppermute x3, starting transfers between devices, one_round(): lax.ppermute(own, AXES, among_left(d))  9.22 us
    ppermute x3, starting transfers between devices, one_round(): lax.ppermute(left_out[d], AXES, among_left(d))  9.21 us
    ppermute x2, waiting for transfers between devices, one_round(): rights = [lax.ppermute(own, AXES, to_left(m)) for m in range(far)]  8.38 us
    ppermute x3, waiting for transfers between devices, one_round(): lax.ppermute(own, AXES, among_left(d))  5.6 us
    pallas_call x1, Pallas kernels, tile(): pl.pallas_call(functools.partial(tile_kernel, near, far, people_all, math...  3.15 us
    ppermute x3, waiting for transfers between devices, one_round(): lax.ppermute(left_out[d], AXES, among_left(d))  3.03 us
    ppermute x2, starting transfers between devices, one_round(): lax.ppermute(right_out[m], AXES, from_left(m))  2.59 us
  transfers between devices with their start and end apart: 11, of which 6 were waited for; matrix products, arithmetic and copies ran while one was open for 0% of the time, Pallas kernels for 0%

profile of v1, /device:TPU:0, one launch (start us, length us, event | category | flops | bytes accessed | tf_op | source)
XLA Modules:
  0.0 60.6 jit_solution(16131684116286282996)
XLA Ops:
  0.0 0.0 copy-start.2
  0.0 0.0 copy-start.1
  0.0 0.7 %copy-done.2 = s32[4]{0:T(128)S(1)} copy-done((s32[4]{0:T(128)S(1)}, s32[4]{0:T(128)}, u32[]{:S(2)}) %copy-start.2) | copy-done | bytes 40
  0.7 0.0 copy-done.1
  0.7 59.2 %conditional.1 = (bf16[1,128,1024]{2,1,0:T(8,128)(2,1)S(1)}) conditional(s32[]{:T(128)} %bitcast.30, (bf16[1,128,1536]{2,1,0:T(8,128)(2,1)}, s32[1,1,1536]{2,1,0:T(1,128)S(1)}) %tuple.34, (bf16[1,128,1536]{2,1,0:T(8,128)(2,1)}, s32[1,1,1536]{2,1,0:T(1,128)S(1)}) %tuple.35, (bf16[1,128,1536]{2,1,0:T(8,128)(2,1)}, ...), branch_computations={%region_0.0_spmd, %region_2.0_spmd, %region_4.0_spmd} | conditional | flops 1547 | bytes 10785310 | solution.py:160
  0.7 13.2 %psum.20.refs_6_ = s32[1,1536]{1,0:T(1,128)S(1)} all-reduce(s32[1,1536]{1,0:T(1,128)S(1)} %bitcast.70), channel_id=1, replica_groups=mesh['cohort'=4,'person'=8] {'person'}, use_global_device_ids=true, to_apply=%region_5.0 | all-reduce | flops 1536 | bytes 12288 | tf_op jit(solution)/shard_map/cond/branch_2_fun/psum | solution.py:142
  14.0 1.3 %collective-permute-start.27 = (s32[1,1536]{1,0:T(1,128)S(1)}, s32[1,1536]{1,0:T(1,128)S(1)}, u32[]{:S(2)}, u32[]{:S(2)}) collective-permute-start(s32[1,1536]{1,0:T(1,128)S(1)} %psum.20.refs_6_), channel_id=1, source_target_pairs={{24,0},{25,1},{26,2},{27,3},{28,4},{29,5},{30,6},{31,7},{8,16},{9,... | collective-permute-start | bytes 18440 | tf_op jit(solution)/shard_map/cond/branch_2_fun/ppermute | solution.py:143
  15.3 3.4 %collective-permute-start.22 = (bf16[128,1536]{1,0:T(8,128)(2,1)}, bf16[128,1536]{1,0:T(8,128)(2,1)S(1)}, u32[]{:S(2)}, u32[]{:S(2)}) collective-permute-start(bf16[128,1536]{1,0:T(8,128)(2,1)} %bitcast.62), channel_id=1, source_target_pairs={{0,1},{1,0},{2,3},{3,2},{4,5},{5,4},{6,7},{7,6},{16,17},{17,16},{1... | collective-permute-start | bytes 1179656 | tf_op jit(solution)/shard_map/cond/branch_2_fun/ppermute | solution.py:140
  18.7 2.4 %collective-permute-start.23 = (bf16[128,1536]{1,0:T(8,128)(2,1)}, bf16[128,1536]{1,0:T(8,128)(2,1)S(1)}, u32[]{:S(2)}, u32[]{:S(2)}) collective-permute-start(bf16[128,1536]{1,0:T(8,128)(2,1)} %bitcast.63), channel_id=1, source_target_pairs={{0,2},{1,3},{2,0},{3,1},{4,6},{5,7},{6,4},{7,5},{16,18},{17,19},{1... | collective-permute-start | bytes 1179656 | tf_op jit(solution)/shard_map/cond/branch_2_fun/ppermute | solution.py:140
  21.1 3.4 %collective-permute-start.24 = (bf16[128,1536]{1,0:T(8,128)(2,1)}, bf16[128,1536]{1,0:T(8,128)(2,1)S(1)}, u32[]{:S(2)}, u32[]{:S(2)}) collective-permute-start(bf16[128,1536]{1,0:T(8,128)(2,1)} %bitcast.64), channel_id=1, source_target_pairs={{0,3},{1,2},{2,1},{3,0},{4,7},{5,6},{6,5},{7,4},{16,19},{17,18},{1... | collective-permute-start | bytes 1179656 | tf_op jit(solution)/shard_map/cond/branch_2_fun/ppermute | solution.py:140
  24.5 1.3 %collective-permute-start.25 = (bf16[128,1536]{1,0:T(8,128)(2,1)}, bf16[128,1536]{1,0:T(8,128)(2,1)S(1)}, u32[]{:S(2)}, u32[]{:S(2)}) collective-permute-start(bf16[128,1536]{1,0:T(8,128)(2,1)} %bitcast.65), channel_id=1, source_target_pairs={{24,0},{25,1},{26,2},{27,3},{28,4},{29,5},{30,6},{31,7},{8,16},{9,... | collective-permute-start | bytes 1179656 | tf_op jit(solution)/shard_map/cond/branch_2_fun/ppermute | solution.py:141
  25.8 0.0 collective-permute-done.27.refs_7_
  25.8 1.3 %collective-permute-start.26 = (bf16[128,1536]{1,0:T(8,128)(2,1)}, bf16[128,1536]{1,0:T(8,128)(2,1)S(1)}, u32[]{:S(2)}, u32[]{:S(2)}) collective-permute-start(bf16[128,1536]{1,0:T(8,128)(2,1)} %bitcast.66), channel_id=1, source_target_pairs={{28,0},{29,1},{30,2},{31,3},{24,4},{25,5},{26,6},{27,7},{12,16},{1... | collective-permute-start | bytes 1179656 | tf_op jit(solution)/shard_map/cond/branch_2_fun/ppermute | solution.py:141
  27.1 0.0 collective-permute-done.22.refs_1_
  27.1 1.5 %collective-permute-done.23.refs_2_ = bf16[128,1536]{1,0:T(8,128)(2,1)S(1)} collective-permute-done((bf16[128,1536]{1,0:T(8,128)(2,1)}, bf16[128,1536]{1,0:T(8,128)(2,1)S(1)}, u32[]{:S(2)}, u32[]{:S(2)}) %collective-permute-start.23) | collective-permute-done | bytes 393248 | tf_op jit(solution)/shard_map/cond/branch_2_fun/ppermute | solution.py:140
  28.6 4.1 %collective-permute-done.24.refs_3_ = bf16[128,1536]{1,0:T(8,128)(2,1)S(1)} collective-permute-done((bf16[128,1536]{1,0:T(8,128)(2,1)}, bf16[128,1536]{1,0:T(8,128)(2,1)S(1)}, u32[]{:S(2)}, u32[]{:S(2)}) %collective-permute-start.24) | collective-permute-done | bytes 393248 | tf_op jit(solution)/shard_map/cond/branch_2_fun/ppermute | solution.py:140
  32.7 2.0 %collective-permute-done.25.refs_4_ = bf16[128,1536]{1,0:T(8,128)(2,1)S(1)} collective-permute-done((bf16[128,1536]{1,0:T(8,128)(2,1)}, bf16[128,1536]{1,0:T(8,128)(2,1)S(1)}, u32[]{:S(2)}, u32[]{:S(2)}) %collective-permute-start.25) | collective-permute-done | bytes 393248 | tf_op jit(solution)/shard_map/cond/branch_2_fun/ppermute | solution.py:141
  34.7 6.4 %collective-permute-done.26.refs_5_ = bf16[128,1536]{1,0:T(8,128)(2,1)S(1)} collective-permute-done((bf16[128,1536]{1,0:T(8,128)(2,1)}, bf16[128,1536]{1,0:T(8,128)(2,1)S(1)}, u32[]{:S(2)}, u32[]{:S(2)}) %collective-permute-start.26) | collective-permute-done | bytes 393248 | tf_op jit(solution)/shard_map/cond/branch_2_fun/ppermute | solution.py:141
  41.1 3.2 %branch_2_fun.2 = (bf16[4,128,256]{2,1,0:T(8,128)(2,1)S(1)}, bf16[2,128,512]{2,1,0:T(8,128)(2,1)S(1)}) custom-call(bf16[128,1536]{1,0:T(8,128)(2,1)} %bitcast.67, bf16[128,1536]{1,0:T(8,128)(2,1)S(1)} %collective-permute-done.22.refs_1_, bf16[128,1536]{1,0:T(8,128)(2,1)S(1)} %collective-permute-done.23.refs_2_, ...), custom_call_target="tpu_custom_call" | custom-call | tf_op jit(solution)/shard_map/cond/branch_2_fun/pallas_call | solution.py:70
  44.3 1.3 %collective-permute-start.31 = (bf16[128,512]{1,0:T(8,128)(2,1)S(1)}, bf16[128,512]{1,0:T(8,128)(2,1)S(1)}, u32[]{:S(2)}, u32[]{:S(2)}) collective-permute-start(bf16[128,512]{1,0:T(8,128)(2,1)S(1)} %get-tuple-element.47), channel_id=1, source_target_pairs={{0,24},{1,25},{2,26},{3,27},{4,28},{5,29},{6,30},{7,31},{16,8},{17... | collective-permute-start | bytes 393224 | tf_op jit(solution)/shard_map/cond/branch_2_fun/ppermute | solution.py:148
  45.6 1.3 %collective-permute-start.32 = (bf16[128,512]{1,0:T(8,128)(2,1)S(1)}, bf16[128,512]{1,0:T(8,128)(2,1)S(1)}, u32[]{:S(2)}, u32[]{:S(2)}) collective-permute-start(bf16[128,512]{1,0:T(8,128)(2,1)S(1)} %get-tuple-element.46), channel_id=1, source_target_pairs={{0,28},{1,29},{2,30},{3,31},{4,24},{5,25},{6,26},{7,27},{16,12},{1... | collective-permute-start | bytes 393224 | tf_op jit(solution)/shard_map/cond/branch_2_fun/ppermute | solution.py:148
  46.9 3.4 %collective-permute-start.28 = (bf16[128,256]{1,0:T(8,128)(2,1)S(1)}, bf16[128,256]{1,0:T(8,128)(2,1)S(1)}, u32[]{:S(2)}, u32[]{:S(2)}) collective-permute-start(bf16[128,256]{1,0:T(8,128)(2,1)S(1)} %get-tuple-element.50), channel_id=1, source_target_pairs={{0,1},{1,0},{2,3},{3,2},{4,5},{5,4},{6,7},{7,6},{16,17},{17,16},{1... | collective-permute-start | bytes 196616 | tf_op jit(solution)/shard_map/cond/branch_2_fun/ppermute | solution.py:146
  50.3 1.9 %collective-permute-start.29 = (bf16[128,256]{1,0:T(8,128)(2,1)S(1)}, bf16[128,256]{1,0:T(8,128)(2,1)S(1)}, u32[]{:S(2)}, u32[]{:S(2)}) collective-permute-start(bf16[128,256]{1,0:T(8,128)(2,1)S(1)} %get-tuple-element.49), channel_id=1, source_target_pairs={{0,2},{1,3},{2,0},{3,1},{4,6},{5,7},{6,4},{7,5},{16,18},{17,19},{1... | collective-permute-start | bytes 196616 | tf_op jit(solution)/shard_map/cond/branch_2_fun/ppermute | solution.py:146
  52.2 3.9 %collective-permute-start.30 = (bf16[128,256]{1,0:T(8,128)(2,1)S(1)}, bf16[128,256]{1,0:T(8,128)(2,1)S(1)}, u32[]{:S(2)}, u32[]{:S(2)}) collective-permute-start(bf16[128,256]{1,0:T(8,128)(2,1)S(1)} %get-tuple-element.48), channel_id=1, source_target_pairs={{0,3},{1,2},{2,1},{3,0},{4,7},{5,6},{6,5},{7,4},{16,19},{17,18},{1... | collective-permute-start | bytes 196616 | tf_op jit(solution)/shard_map/cond/branch_2_fun/ppermute | solution.py:146
  56.2 0.1 pad_add_fusion.2.where_ref
  56.3 0.0 collective-permute-done.28.refs_1_
  56.3 0.2 collective-permute-done.29.refs_2_
  56.5 2.8 %collective-permute-done.30.refs_3_ = bf16[128,256]{1,0:T(8,128)(2,1)S(1)} collective-permute-done((bf16[128,256]{1,0:T(8,128)(2,1)S(1)}, bf16[128,256]{1,0:T(8,128)(2,1)S(1)}, u32[]{:S(2)}, u32[]{:S(2)}) %collective-permute-start.30) | collective-permute-done | bytes 65568 | tf_op jit(solution)/shard_map/cond/branch_2_fun/ppermute | solution.py:146
  59.3 0.0 collective-permute-done.31.refs_4_
  59.3 0.0 collective-permute-done.32.refs_5_
  59.3 0.6 %branch_2_fun.3 = bf16[1,128,1024]{2,1,0:T(8,128)(2,1)S(1)} custom-call(s32[2]{0:T(128)S(1)} %pad_add_fusion.2.where_ref, bf16[128,256]{1,0:T(8,128)(2,1)S(1)} %get-tuple-element.51.refs_0_, bf16[128,256]{1,0:T(8,128)(2,1)S(1)} %collective-permute-done.28.refs_1_, bf16[128,256]{1,0:T(8,128)(2,1)S(1)} %collective-permute-done.29.refs_2_, ...), custom_call_target="tpu_custom_call" | custom-call | tf_op jit(solution)/shard_map/cond/branch_2_fun/pallas_call | solution.py:111
  59.9 0.0 copy-start
  59.9 0.7 %copy-done = bf16[1,128,1024]{2,1,0:T(8,128)(2,1)} copy-done((bf16[1,128,1024]{2,1,0:T(8,128)(2,1)}, bf16[1,128,1024]{2,1,0:T(8,128)(2,1)S(1)}, u32[]{:S(2)}) %copy-start) | copy-done | bytes 262168
  (2 shorter events, 0.0 us)
Async XLA Ops:
  0.0 0.7 %copy-start.2 = (s32[4]{0:T(128)S(1)}, s32[4]{0:T(128)}, u32[]{:S(2)}) copy-start(s32[4]{0:T(128)} %param.8) | copy-start | bytes 52
  0.0 0.7 %copy-start.1 = (s32[1,1,1536]{2,1,0:T(1,128)S(1)}, s32[1,1,1536]{2,1,0:T(1,128)}, u32[]{:S(2)}) copy-start(s32[1,1,1536]{2,1,0:T(1,128)} %param.7) | copy-start | bytes 18436
  14.0 11.8 %collective-permute-start.27 = (s32[1,1536]{1,0:T(1,128)S(1)}, s32[1,1536]{1,0:T(1,128)S(1)}, u32[]{:S(2)}, u32[]{:S(2)}) collective-permute-start(s32[1,1536]{1,0:T(1,128)S(1)} %psum.20.refs_6_), channel_id=1, source_target_pairs={{24,0},{25,1},{26,2},{27,3},{28,4},{29,5},{30,6},{31,7},{8,16},{9,... | collective-permute-start | bytes 18440 | tf_op jit(solution)/shard_map/cond/branch_2_fun/ppermute | solution.py:143
  15.3 11.9 %collective-permute-start.22 = (bf16[128,1536]{1,0:T(8,128)(2,1)}, bf16[128,1536]{1,0:T(8,128)(2,1)S(1)}, u32[]{:S(2)}, u32[]{:S(2)}) collective-permute-start(bf16[128,1536]{1,0:T(8,128)(2,1)} %bitcast.62), channel_id=1, source_target_pairs={{0,1},{1,0},{2,3},{3,2},{4,5},{5,4},{6,7},{7,6},{16,17},{17,16},{1... | collective-permute-start | bytes 1179656 | tf_op jit(solution)/shard_map/cond/branch_2_fun/ppermute | solution.py:140
  18.7 9.9 %collective-permute-start.23 = (bf16[128,1536]{1,0:T(8,128)(2,1)}, bf16[128,1536]{1,0:T(8,128)(2,1)S(1)}, u32[]{:S(2)}, u32[]{:S(2)}) collective-permute-start(bf16[128,1536]{1,0:T(8,128)(2,1)} %bitcast.63), channel_id=1, source_target_pairs={{0,2},{1,3},{2,0},{3,1},{4,6},{5,7},{6,4},{7,5},{16,18},{17,19},{1... | collective-permute-start | bytes 1179656 | tf_op jit(solution)/shard_map/cond/branch_2_fun/ppermute | solution.py:140
  21.1 11.7 %collective-permute-start.24 = (bf16[128,1536]{1,0:T(8,128)(2,1)}, bf16[128,1536]{1,0:T(8,128)(2,1)S(1)}, u32[]{:S(2)}, u32[]{:S(2)}) collective-permute-start(bf16[128,1536]{1,0:T(8,128)(2,1)} %bitcast.64), channel_id=1, source_target_pairs={{0,3},{1,2},{2,1},{3,0},{4,7},{5,6},{6,5},{7,4},{16,19},{17,18},{1... | collective-permute-start | bytes 1179656 | tf_op jit(solution)/shard_map/cond/branch_2_fun/ppermute | solution.py:140
  24.5 10.2 %collective-permute-start.25 = (bf16[128,1536]{1,0:T(8,128)(2,1)}, bf16[128,1536]{1,0:T(8,128)(2,1)S(1)}, u32[]{:S(2)}, u32[]{:S(2)}) collective-permute-start(bf16[128,1536]{1,0:T(8,128)(2,1)} %bitcast.65), channel_id=1, source_target_pairs={{24,0},{25,1},{26,2},{27,3},{28,4},{29,5},{30,6},{31,7},{8,16},{9,... | collective-permute-start | bytes 1179656 | tf_op jit(solution)/shard_map/cond/branch_2_fun/ppermute | solution.py:141
  25.8 15.3 %collective-permute-start.26 = (bf16[128,1536]{1,0:T(8,128)(2,1)}, bf16[128,1536]{1,0:T(8,128)(2,1)S(1)}, u32[]{:S(2)}, u32[]{:S(2)}) collective-permute-start(bf16[128,1536]{1,0:T(8,128)(2,1)} %bitcast.66), channel_id=1, source_target_pairs={{28,0},{29,1},{30,2},{31,3},{24,4},{25,5},{26,6},{27,7},{12,16},{1... | collective-permute-start | bytes 1179656 | tf_op jit(solution)/shard_map/cond/branch_2_fun/ppermute | solution.py:141
  44.3 15.0 %collective-permute-start.31 = (bf16[128,512]{1,0:T(8,128)(2,1)S(1)}, bf16[128,512]{1,0:T(8,128)(2,1)S(1)}, u32[]{:S(2)}, u32[]{:S(2)}) collective-permute-start(bf16[128,512]{1,0:T(8,128)(2,1)S(1)} %get-tuple-element.47), channel_id=1, source_target_pairs={{0,24},{1,25},{2,26},{3,27},{4,28},{5,29},{6,30},{7,31},{16,8},{17... | collective-permute-start | bytes 393224 | tf_op jit(solution)/shard_map/cond/branch_2_fun/ppermute | solution.py:148
  45.6 13.7 %collective-permute-start.32 = (bf16[128,512]{1,0:T(8,128)(2,1)S(1)}, bf16[128,512]{1,0:T(8,128)(2,1)S(1)}, u32[]{:S(2)}, u32[]{:S(2)}) collective-permute-start(bf16[128,512]{1,0:T(8,128)(2,1)S(1)} %get-tuple-element.46), channel_id=1, source_target_pairs={{0,28},{1,29},{2,30},{3,31},{4,24},{5,25},{6,26},{7,27},{16,12},{1... | collective-permute-start | bytes 393224 | tf_op jit(solution)/shard_map/cond/branch_2_fun/ppermute | solution.py:148
  46.9 9.3 %collective-permute-start.28 = (bf16[128,256]{1,0:T(8,128)(2,1)S(1)}, bf16[128,256]{1,0:T(8,128)(2,1)S(1)}, u32[]{:S(2)}, u32[]{:S(2)}) collective-permute-start(bf16[128,256]{1,0:T(8,128)(2,1)S(1)} %get-tuple-element.50), channel_id=1, source_target_pairs={{0,1},{1,0},{2,3},{3,2},{4,5},{5,4},{6,7},{7,6},{16,17},{17,16},{1... | collective-permute-start | bytes 196616 | tf_op jit(solution)/shard_map/cond/branch_2_fun/ppermute | solution.py:146
  50.3 6.2 %collective-permute-start.29 = (bf16[128,256]{1,0:T(8,128)(2,1)S(1)}, bf16[128,256]{1,0:T(8,128)(2,1)S(1)}, u32[]{:S(2)}, u32[]{:S(2)}) collective-permute-start(bf16[128,256]{1,0:T(8,128)(2,1)S(1)} %get-tuple-element.49), channel_id=1, source_target_pairs={{0,2},{1,3},{2,0},{3,1},{4,6},{5,7},{6,4},{7,5},{16,18},{17,19},{1... | collective-permute-start | bytes 196616 | tf_op jit(solution)/shard_map/cond/branch_2_fun/ppermute | solution.py:146
  52.2 7.1 %collective-permute-start.30 = (bf16[128,256]{1,0:T(8,128)(2,1)S(1)}, bf16[128,256]{1,0:T(8,128)(2,1)S(1)}, u32[]{:S(2)}, u32[]{:S(2)}) collective-permute-start(bf16[128,256]{1,0:T(8,128)(2,1)S(1)} %get-tuple-element.48), channel_id=1, source_target_pairs={{0,3},{1,2},{2,1},{3,0},{4,7},{5,6},{6,5},{7,4},{16,19},{17,18},{1... | collective-permute-start | bytes 196616 | tf_op jit(solution)/shard_map/cond/branch_2_fun/ppermute | solution.py:146
  59.9 0.7 %copy-start = (bf16[1,128,1024]{2,1,0:T(8,128)(2,1)}, bf16[1,128,1024]{2,1,0:T(8,128)(2,1)S(1)}, u32[]{:S(2)}) copy-start(bf16[1,128,1024]{2,1,0:T(8,128)(2,1)S(1)} %get-tuple-element.106) | copy-start | bytes 786436

commit v2 on v1

--- a/solution.py
+++ b/solution.py
@@ -125,23 +125,29 @@
     left = left_cohorts(cohorts, round_number)
 
     def among_left(d):
-        return [(c * blocks + i, c * blocks + (i ^ d)) for c in left for i in range(blocks)]
+        return [
+            (c * blocks + i, c * blocks + (i ^ d if c in left else i))
+            for c in range(cohorts)
+            for i in range(blocks)
+        ]
 
     def to_left(m):
-        return [
-            ((c ^ round_number) * blocks + (i ^ near * m), c * blocks + i)
-            for c in left
-            for i in range(blocks)
-        ]
+        pairs = []
+        for c in left:
+            for i in range(blocks):
+                pairs.append(((c ^ round_number) * blocks + (i ^ near * m), c * blocks + i))
+                pairs.append((c * blocks + i, (c ^ 1) * blocks + i))
+        return pairs
 
     def from_left(m):
         return [(b, a) for a, b in to_left(m)]
 
+    swap = [(c, c ^ round_number) for c in range(cohorts)]
+    partner_counts = lax.ppermute(allele_counts[0], "cohort", swap)
     lefts = [own] + [lax.ppermute(own, AXES, among_left(d)) for d in range(1, near)]
     rights = [lax.ppermute(own, AXES, to_left(m)) for m in range(far)]
-    totals = lax.psum(allele_counts[0], "person")
-    right_totals = lax.ppermute(totals, AXES, to_left(0))
-    left_out, right_out = tile(lefts, rights, totals, right_totals, people_all)
+    totals = lax.psum(jnp.concatenate([allele_counts[0], partner_counts]), "person")
+    left_out, right_out = tile(lefts, rights, totals[:1], totals[1:], people_all)
     left_parts = [left_out[0]] + [
         lax.ppermute(left_out[d], AXES, among_left(d)) for d in range(1, near)
     ]

time: 61.1 us -> 71.3 us (1.17)
  blocking collectives: 13.2 us -> 41.1 us
  waiting for transfers between devices: 17 us -> 2.17 us
  starting transfers between devices: 24.9 us -> 21.7 us
    psum x1, blocking collectives: 13.2 us -> 41.1 us  [one_round(): lax.psum(jnp.concatenate([allele_counts[0], partner_counts]), 'person')]
    ppermute x2, waiting for transfers between devices: 8.38 us -> 0.01 us  [one_round(): rights = [lax.ppermute(own, AXES, to_left(m)) for m in range(far)]]
    ppermute x3, waiting for transfers between devices: 5.6 us -> 0.01 us  [one_round(): lax.ppermute(own, AXES, among_left(d))]
    ppermute x2, starting transfers between devices: 2.59 us -> 0.12 us  [one_round(): lax.ppermute(right_out[m], AXES, from_left(m))]
    ppermute x2, starting transfers between devices: 2.58 us -> 0.73 us  [one_round(): rights = [lax.ppermute(own, AXES, to_left(m)) for m in range(far)]]
    ppermute x1, starting transfers between devices: 1.28 us -> 2.44 us  [one_round(): partner_counts = lax.ppermute(allele_counts[0], 'cohort', swap)]
    ppermute x3, waiting for transfers between devices: 3.03 us -> 2.15 us  [one_round(): lax.ppermute(left_out[d], AXES, among_left(d))]
  transfers between devices with their start and end apart: 11 -> 11, of which waited for: 6 -> 1; matrix products, arithmetic and copies ran while one was open for 0% -> 0% of each run, Pallas kernels for 0% -> 0%
where the time goes in v2:
time: 71.3 us; the launch traced here: 70.6 us
  blocking collectives  41.1 us (58%)
  starting transfers between devices  21.7 us (30%)
  Pallas kernels  3.77 us (5%)
  waiting for transfers between devices  2.17 us (3%)
  local copies, waits for them, and re-layouts  1.41 us (2%)
    psum x1, blocking collectives, one_round(): lax.psum(jnp.concatenate([allele_counts[0], partner_counts]), 'person')  41.1 us
    ppermute x3, starting transfers between devices, one_round(): lax.ppermute(left_out[d], AXES, among_left(d))  9.21 us
    ppermute x3, starting transfers between devices, one_round(): lax.ppermute(own, AXES, among_left(d))  9.21 us
    pallas_call x1, Pallas kernels, tile(): pl.pallas_call(functools.partial(tile_kernel, near, far, people_all, math...  3.16 us
    ppermute x1, starting transfers between devices, one_round(): partner_counts = lax.ppermute(allele_counts[0], 'cohort', swap)  2.44 us
    ppermute x3, waiting for transfers between devices, one_round(): lax.ppermute(left_out[d], AXES, among_left(d))  2.15 us
  transfers between devices with their start and end apart: 11, of which 1 were waited for; matrix products, arithmetic and copies ran while one was open for 0% of the time, Pallas kernels for 0%

profile of v2, /device:TPU:0, one launch (start us, length us, event | category | flops | bytes accessed | tf_op | source)
XLA Modules:
  0.0 70.6 jit_solution(4542310128083956716)
XLA Ops:
  0.0 0.0 copy-start.2
  0.0 0.0 copy-start.1
  0.0 0.7 copy-done.2
  0.7 0.0 copy-done.1
  0.7 69.1 %conditional.1 = (bf16[1,128,1024]{2,1,0:T(8,128)(2,1)S(1)}) conditional(s32[]{:T(128)} %bitcast.30, (bf16[1,128,1536]{2,1,0:T(8,128)(2,1)}, s32[1,1,1536]{2,1,0:T(1,128)S(1)}) %tuple.37, (bf16[1,128,1536]{2,1,0:T(8,128)(2,1)}, s32[1,1,1536]{2,1,0:T(1,128)S(1)}) %tuple.38, (bf16[1,128,1536]{2,1,0:T(8,128)(2,1)}, ...), branch_computations={%region_0.0_spmd, %region_2.0_spmd, %region_4.0_spmd} | conditional | flops 6155 | bytes 10846750 | solution.py:166
  0.7 2.4 %collective-permute-start.27 = (s32[1,1536]{1,0:T(1,128)S(1)}, s32[1,1536]{1,0:T(1,128)S(1)}, u32[]{:S(2)}, u32[]{:S(2)}) collective-permute-start(s32[1,1536]{1,0:T(1,128)S(1)} %bitcast.72), channel_id=1, source_target_pairs={{0,24},{8,16},{16,8},{24,0},{1,25},{9,17},{17,9},{25,1},{2,26},{10... | collective-permute-start | bytes 18440 | tf_op jit(solution)/shard_map/cond/branch_2_fun/ppermute | solution.py:146
  3.2 3.4 %collective-permute-start.22 = (bf16[128,1536]{1,0:T(8,128)(2,1)}, bf16[128,1536]{1,0:T(8,128)(2,1)S(1)}, u32[]{:S(2)}, u32[]{:S(2)}) collective-permute-start(bf16[128,1536]{1,0:T(8,128)(2,1)} %bitcast.62), channel_id=1, source_target_pairs={{0,1},{1,0},{2,3},{3,2},{4,5},{5,4},{6,7},{7,6},{8,8},{9,9},{10,10... | collective-permute-start | bytes 1179656 | tf_op jit(solution)/shard_map/cond/branch_2_fun/ppermute | solution.py:147
  6.6 3.5 %collective-permute-start.23 = (bf16[128,1536]{1,0:T(8,128)(2,1)}, bf16[128,1536]{1,0:T(8,128)(2,1)S(1)}, u32[]{:S(2)}, u32[]{:S(2)}) collective-permute-start(bf16[128,1536]{1,0:T(8,128)(2,1)} %bitcast.63), channel_id=1, source_target_pairs={{0,2},{1,3},{2,0},{3,1},{4,6},{5,7},{6,4},{7,5},{8,8},{9,9},{10,10... | collective-permute-start | bytes 1179656 | tf_op jit(solution)/shard_map/cond/branch_2_fun/ppermute | solution.py:147
  10.1 2.3 %collective-permute-start.24 = (bf16[128,1536]{1,0:T(8,128)(2,1)}, bf16[128,1536]{1,0:T(8,128)(2,1)S(1)}, u32[]{:S(2)}, u32[]{:S(2)}) collective-permute-start(bf16[128,1536]{1,0:T(8,128)(2,1)} %bitcast.64), channel_id=1, source_target_pairs={{0,3},{1,2},{2,1},{3,0},{4,7},{5,6},{6,5},{7,4},{8,8},{9,9},{10,10... | collective-permute-start | bytes 1179656 | tf_op jit(solution)/shard_map/cond/branch_2_fun/ppermute | solution.py:147
  12.4 0.1 collective-permute-start.25
  12.5 0.0 collective-permute-done.27
  12.5 0.7 collective-permute-start.26
  13.2 41.1 %psum.20 = s32[2,1536]{1,0:T(2,128)S(1)} all-reduce(s32[2,1536]{1,0:T(2,128)S(1)} %pad_add_fusion.4), channel_id=1, replica_groups=mesh['cohort'=4,'person'=8] {'person'}, use_global_device_ids=true, to_apply=%region_5.0 | all-reduce | flops 3072 | bytes 24576 | tf_op jit(solution)/shard_map/cond/branch_2_fun/psum | solution.py:149
  54.3 0.0 collective-permute-done.22.refs_1_
  54.4 0.0 collective-permute-done.23.refs_2_
  54.4 0.0 collective-permute-done.24.refs_3_
  54.4 0.0 collective-permute-done.25.refs_4_
  54.4 0.0 collective-permute-done.26.refs_5_
  54.4 3.2 %branch_2_fun.2 = (bf16[4,128,256]{2,1,0:T(8,128)(2,1)S(1)}, bf16[2,128,512]{2,1,0:T(8,128)(2,1)S(1)}) custom-call(bf16[128,1536]{1,0:T(8,128)(2,1)} %bitcast.67, bf16[128,1536]{1,0:T(8,128)(2,1)S(1)} %collective-permute-done.22.refs_1_, bf16[128,1536]{1,0:T(8,128)(2,1)S(1)} %collective-permute-done.23.refs_2_, ...), custom_call_target="tpu_custom_call" | custom-call | tf_op jit(solution)/shard_map/cond/branch_2_fun/pallas_call | solution.py:70
  57.6 0.1 collective-permute-start.31
  57.7 0.1 collective-permute-start.32
  57.8 1.9 %collective-permute-start.28 = (bf16[128,256]{1,0:T(8,128)(2,1)S(1)}, bf16[128,256]{1,0:T(8,128)(2,1)S(1)}, u32[]{:S(2)}, u32[]{:S(2)}) collective-permute-start(bf16[128,256]{1,0:T(8,128)(2,1)S(1)} %get-tuple-element.54), channel_id=1, source_target_pairs={{0,1},{1,0},{2,3},{3,2},{4,5},{5,4},{6,7},{7,6},{8,8},{9,9},{10,10... | collective-permute-start | bytes 196616 | tf_op jit(solution)/shard_map/cond/branch_2_fun/ppermute | solution.py:152
  59.7 2.0 %collective-permute-start.29 = (bf16[128,256]{1,0:T(8,128)(2,1)S(1)}, bf16[128,256]{1,0:T(8,128)(2,1)S(1)}, u32[]{:S(2)}, u32[]{:S(2)}) collective-permute-start(bf16[128,256]{1,0:T(8,128)(2,1)S(1)} %get-tuple-element.53), channel_id=1, source_target_pairs={{0,2},{1,3},{2,0},{3,1},{4,6},{5,7},{6,4},{7,5},{8,8},{9,9},{10,10... | collective-permute-start | bytes 196616 | tf_op jit(solution)/shard_map/cond/branch_2_fun/ppermute | solution.py:152
  61.7 5.3 %collective-permute-start.30 = (bf16[128,256]{1,0:T(8,128)(2,1)S(1)}, bf16[128,256]{1,0:T(8,128)(2,1)S(1)}, u32[]{:S(2)}, u32[]{:S(2)}) collective-permute-start(bf16[128,256]{1,0:T(8,128)(2,1)S(1)} %get-tuple-element.52), channel_id=1, source_target_pairs={{0,3},{1,2},{2,1},{3,0},{4,7},{5,6},{6,5},{7,4},{8,8},{9,9},{10,10... | collective-permute-start | bytes 196616 | tf_op jit(solution)/shard_map/cond/branch_2_fun/ppermute | solution.py:152
  67.0 0.1 pad_add_fusion.5.where_ref
  67.1 0.0 collective-permute-done.28.refs_1_
  67.1 0.0 collective-permute-done.29.refs_2_
  67.1 2.1 %collective-permute-done.30.refs_3_ = bf16[128,256]{1,0:T(8,128)(2,1)S(1)} collective-permute-done((bf16[128,256]{1,0:T(8,128)(2,1)S(1)}, bf16[128,256]{1,0:T(8,128)(2,1)S(1)}, u32[]{:S(2)}, u32[]{:S(2)}) %collective-permute-start.30) | collective-permute-done | bytes 65568 | tf_op jit(solution)/shard_map/cond/branch_2_fun/ppermute | solution.py:152
  69.2 0.0 collective-permute-done.31.refs_4_
  69.2 0.0 collective-permute-done.32.refs_5_
  69.2 0.6 branch_2_fun.3
  69.8 0.0 copy-start
  69.9 0.7 copy-done
  (4 shorter events, 0.1 us)
Async XLA Ops:
  0.0 0.7 copy-start.2
  0.0 0.7 copy-start.1
  0.7 11.8 %collective-permute-start.27 = (s32[1,1536]{1,0:T(1,128)S(1)}, s32[1,1536]{1,0:T(1,128)S(1)}, u32[]{:S(2)}, u32[]{:S(2)}) collective-permute-start(s32[1,1536]{1,0:T(1,128)S(1)} %bitcast.72), channel_id=1, source_target_pairs={{0,24},{8,16},{16,8},{24,0},{1,25},{9,17},{17,9},{25,1},{2,26},{10... | collective-permute-start | bytes 18440 | tf_op jit(solution)/shard_map/cond/branch_2_fun/ppermute | solution.py:146
  3.2 51.2 %collective-permute-start.22 = (bf16[128,1536]{1,0:T(8,128)(2,1)}, bf16[128,1536]{1,0:T(8,128)(2,1)S(1)}, u32[]{:S(2)}, u32[]{:S(2)}) collective-permute-start(bf16[128,1536]{1,0:T(8,128)(2,1)} %bitcast.62), channel_id=1, source_target_pairs={{0,1},{1,0},{2,3},{3,2},{4,5},{5,4},{6,7},{7,6},{8,8},{9,9},{10,10... | collective-permute-start | bytes 1179656 | tf_op jit(solution)/shard_map/cond/branch_2_fun/ppermute | solution.py:147
  6.6 47.7 %collective-permute-start.23 = (bf16[128,1536]{1,0:T(8,128)(2,1)}, bf16[128,1536]{1,0:T(8,128)(2,1)S(1)}, u32[]{:S(2)}, u32[]{:S(2)}) collective-permute-start(bf16[128,1536]{1,0:T(8,128)(2,1)} %bitcast.63), channel_id=1, source_target_pairs={{0,2},{1,3},{2,0},{3,1},{4,6},{5,7},{6,4},{7,5},{8,8},{9,9},{10,10... | collective-permute-start | bytes 1179656 | tf_op jit(solution)/shard_map/cond/branch_2_fun/ppermute | solution.py:147
  10.1 44.3 %collective-permute-start.24 = (bf16[128,1536]{1,0:T(8,128)(2,1)}, bf16[128,1536]{1,0:T(8,128)(2,1)S(1)}, u32[]{:S(2)}, u32[]{:S(2)}) collective-permute-start(bf16[128,1536]{1,0:T(8,128)(2,1)} %bitcast.64), channel_id=1, source_target_pairs={{0,3},{1,2},{2,1},{3,0},{4,7},{5,6},{6,5},{7,4},{8,8},{9,9},{10,10... | collective-permute-start | bytes 1179656 | tf_op jit(solution)/shard_map/cond/branch_2_fun/ppermute | solution.py:147
  12.4 42.0 %collective-permute-start.25 = (bf16[128,1536]{1,0:T(8,128)(2,1)}, bf16[128,1536]{1,0:T(8,128)(2,1)S(1)}, u32[]{:S(2)}, u32[]{:S(2)}) collective-permute-start(bf16[128,1536]{1,0:T(8,128)(2,1)} %bitcast.65), channel_id=1, source_target_pairs={{24,0},{0,8},{25,1},{1,9},{26,2},{2,10},{27,3},{3,11},{28,4},{4,12... | collective-permute-start | bytes 1179656 | tf_op jit(solution)/shard_map/cond/branch_2_fun/ppermute | solution.py:148
  12.5 41.9 %collective-permute-start.26 = (bf16[128,1536]{1,0:T(8,128)(2,1)}, bf16[128,1536]{1,0:T(8,128)(2,1)S(1)}, u32[]{:S(2)}, u32[]{:S(2)}) collective-permute-start(bf16[128,1536]{1,0:T(8,128)(2,1)} %bitcast.66), channel_id=1, source_target_pairs={{28,0},{0,8},{29,1},{1,9},{30,2},{2,10},{31,3},{3,11},{24,4},{4,12... | collective-permute-start | bytes 1179656 | tf_op jit(solution)/shard_map/cond/branch_2_fun/ppermute | solution.py:148
  57.6 11.6 %collective-permute-start.31 = (bf16[128,512]{1,0:T(8,128)(2,1)S(1)}, bf16[128,512]{1,0:T(8,128)(2,1)S(1)}, u32[]{:S(2)}, u32[]{:S(2)}) collective-permute-start(bf16[128,512]{1,0:T(8,128)(2,1)S(1)} %get-tuple-element.51), channel_id=1, source_target_pairs={{0,24},{8,0},{1,25},{9,1},{2,26},{10,2},{3,27},{11,3},{4,28},{12,4... | collective-permute-start | bytes 393224 | tf_op jit(solution)/shard_map/cond/branch_2_fun/ppermute | solution.py:154
  57.7 11.6 %collective-permute-start.32 = (bf16[128,512]{1,0:T(8,128)(2,1)S(1)}, bf16[128,512]{1,0:T(8,128)(2,1)S(1)}, u32[]{:S(2)}, u32[]{:S(2)}) collective-permute-start(bf16[128,512]{1,0:T(8,128)(2,1)S(1)} %get-tuple-element.50), channel_id=1, source_target_pairs={{0,28},{8,0},{1,29},{9,1},{2,30},{10,2},{3,31},{11,3},{4,24},{12,4... | collective-permute-start | bytes 393224 | tf_op jit(solution)/shard_map/cond/branch_2_fun/ppermute | solution.py:154
  57.8 9.3 %collective-permute-start.28 = (bf16[128,256]{1,0:T(8,128)(2,1)S(1)}, bf16[128,256]{1,0:T(8,128)(2,1)S(1)}, u32[]{:S(2)}, u32[]{:S(2)}) collective-permute-start(bf16[128,256]{1,0:T(8,128)(2,1)S(1)} %get-tuple-element.54), channel_id=1, source_target_pairs={{0,1},{1,0},{2,3},{3,2},{4,5},{5,4},{6,7},{7,6},{8,8},{9,9},{10,10... | collective-permute-start | bytes 196616 | tf_op jit(solution)/shard_map/cond/branch_2_fun/ppermute | solution.py:152
  59.7 7.4 %collective-permute-start.29 = (bf16[128,256]{1,0:T(8,128)(2,1)S(1)}, bf16[128,256]{1,0:T(8,128)(2,1)S(1)}, u32[]{:S(2)}, u32[]{:S(2)}) collective-permute-start(bf16[128,256]{1,0:T(8,128)(2,1)S(1)} %get-tuple-element.53), channel_id=1, source_target_pairs={{0,2},{1,3},{2,0},{3,1},{4,6},{5,7},{6,4},{7,5},{8,8},{9,9},{10,10... | collective-permute-start | bytes 196616 | tf_op jit(solution)/shard_map/cond/branch_2_fun/ppermute | solution.py:152
  61.7 7.6 %collective-permute-start.30 = (bf16[128,256]{1,0:T(8,128)(2,1)S(1)}, bf16[128,256]{1,0:T(8,128)(2,1)S(1)}, u32[]{:S(2)}, u32[]{:S(2)}) collective-permute-start(bf16[128,256]{1,0:T(8,128)(2,1)S(1)} %get-tuple-element.52), channel_id=1, source_target_pairs={{0,3},{1,2},{2,1},{3,0},{4,7},{5,6},{6,5},{7,4},{8,8},{9,9},{10,10... | collective-permute-start | bytes 196616 | tf_op jit(solution)/shard_map/cond/branch_2_fun/ppermute | solution.py:152
  69.8 0.7 copy-start

commit v3 on v0

v3 whole, which is shorter than its diff:
```python
import functools
import math

import jax
import jax.numpy as jnp
from jax import lax
from jax.experimental import pallas as pl
from jax.experimental.pallas import tpu as pltpu
from jax.sharding import PartitionSpec as P

AXES = ("cohort", "person")
VMEM_BYTES = 48 * 1024 * 1024


def left_cohorts(cohorts, round_number):
    if round_number == 1:
        return [c for c in range(cohorts) if c & 1 == 0]
    top = 1 << (round_number.bit_length() - 1)
    return [
        c
        for c in range(cohorts)
        if (c & top == 0 and c & 1 == 0) or (c & top and (c ^ round_number ^ 1) & 1 == 0)
    ]


def half_size(blocks):
    return 1 << (blocks.bit_length() // 2 - 1)


def multiply_kernel(half, root, role_ref, *refs):
    shards, (send_ref, keep_ref) = refs[:-2], refs[-2:]
    own, across = shards[0], shards[1:half]
    crossed, passed = shards[half : 2 * half], shards[2 * half :]
    rows = own.shape[0]

    def product(first, second):
        dims = (((1,), (1,)), ((), ()))
        out = lax.dot_general(first, second, dims, preferred_element_type=jnp.float32)
        return (out / root).astype(jnp.bfloat16)

    def stacked(parts):
        return jnp.concatenate([part[...] for part in parts], axis=0)

    def store(lefts, rights, left_ref, right_ref):
        left_all, right_all = stacked(lefts), stacked(rights)
        by_left = product(left_all, right_all)
        by_right = product(right_all, left_all)
        for t in range(half):
            left_ref[t] = by_left[t * rows : (t + 1) * rows]
            right_ref[t] = by_right[t * rows : (t + 1) * rows]

    @pl.when(role_ref[0] == 1)
    def _():
        rights = (crossed[1], crossed[0]) + crossed[2:]
        store((own,) + across, rights, keep_ref, send_ref)

    @pl.when(role_ref[0] == 0)
    def _():
        store(crossed, (across[0],) + passed, send_ref, keep_ref)


def multiply(role, half, own, across, crossed, passed):
    rows, markers = own.shape
    shards = [own, *across, *crossed, *passed]
    vmem = pl.BlockSpec(memory_space=pltpu.VMEM)
    block = jax.ShapeDtypeStruct((half, rows, half * rows), jnp.bfloat16)
    return pl.pallas_call(
        functools.partial(multiply_kernel, half, math.sqrt(markers)),
        out_shape=(block, block),
        in_specs=[pl.BlockSpec(memory_space=pltpu.SMEM)] + [vmem] * len(shards),
        out_specs=(vmem, vmem),
        compiler_params=pltpu.CompilerParams(vmem_limit_bytes=VMEM_BYTES),
    )(role, *shards)


def place_kernel(half, role_ref, *refs):
    parts, out_ref = refs[:-1], refs[-1]
    rows = out_ref.shape[1]
    near = 2 * half

    def put(offset, value):
        block = jnp.bitwise_xor(role_ref[1], offset)
        out_ref[0, :, pl.ds(pl.multiple_of(block * rows, rows), rows)] = value

    @pl.when(role_ref[0] == 1)
    def _():
        for t in range(half):
            for odd in range(2):
                for m in range(half):
                    put(2 * t + odd + near * m, parts[t][odd, :, m * rows : (m + 1) * rows])

    @pl.when(role_ref[0] == 0)
    def _():
        for t in range(half):
            for even in range(2):
                for s in range(half):
                    put(2 * s + 1 - even + near * t, parts[t][even, :, s * rows : (s + 1) * rows])


def place_blocks(role, half, parts):
    rows = parts[0].shape[1]
    vmem = pl.BlockSpec(memory_space=pltpu.VMEM)
    return pl.pallas_call(
        functools.partial(place_kernel, half),
        out_shape=jax.ShapeDtypeStruct((1, rows, 2 * half * half * rows), jnp.bfloat16),
        in_specs=[pl.BlockSpec(memory_space=pltpu.SMEM)] + [vmem] * len(parts),
        out_specs=vmem,
        compiler_params=pltpu.CompilerParams(vmem_limit_bytes=VMEM_BYTES),
    )(role, *parts)


def one_round(round_number, cohorts, blocks, own):
    half = half_size(blocks)
    near = 2 * half
    left = left_cohorts(cohorts, round_number)

    def send(value, *legs):
        pairs = []
        for c in left:
            for i in range(blocks):
                for leg in legs:
                    (c0, i0), (c1, i1) = leg(c, i)
                    pairs.append((c0 * blocks + i0, c1 * blocks + i1))
        return lax.ppermute(value, AXES, pairs)

    def left_to_left(d):
        return lambda c, i: ((c, i), (c, i ^ d))

    def left_to_mate(d):
        return lambda c, i: ((c, i), (c ^ 1, i ^ d))

    def mate_to_left(d):
        return lambda c, i: ((c ^ 1, i), (c, i ^ d))

    def mate_to_mate(c, i):
        return (c ^ 1, i), (c ^ 1, i)

    def owner_to_left(d):
        return lambda c, i: ((c ^ round_number, i ^ d), (c, i))

    def owner_to_mate(d):
        return lambda c, i: ((c ^ round_number, i ^ d), (c ^ 1, i))

    def mate_to_owner(d):
        return lambda c, i: ((c ^ 1, i), (c ^ round_number, i ^ d))

    cohort = lax.axis_index("cohort")
    is_left = functools.reduce(jnp.logical_or, [cohort == c for c in left])
    role = jnp.stack([is_left.astype(jnp.int32), lax.axis_index("person")])

    across = [send(own, left_to_left(2), owner_to_mate(0))]
    crossed = [send(own, left_to_mate(1), owner_to_left(near))]
    for t in range(2, half):
        across.append(send(own, left_to_left(2 * t), mate_to_mate))
    crossed.append(send(across[0], left_to_mate(1), mate_to_left(0)))
    for t in range(2, half):
        value = jnp.where(is_left, across[t - 1], own)
        crossed.append(send(value, left_to_mate(1), owner_to_left(near * t)))
    passed = [
        send(crossed[0 if m == 1 else m], left_to_mate(0), mate_to_left(0))
        for m in range(1, half)
    ]
    sent, kept = multiply(role, half, own, across, crossed, passed)
    got = send(sent, mate_to_left(1), left_to_mate(0))
    parts = [jnp.stack([kept[t], got[t]]) for t in range(half)]
    for t in range(half):
        if t or round_number != 1:
            parts[t] = send(parts[t], left_to_left(2 * t), mate_to_owner(near * t))
    return place_blocks(role, half, parts)


def standard_rows(rows, counts, people_all):
    totals = lax.psum(counts, "person")
    freq = (totals.astype(jnp.float32) + 1.0) / (2.0 * people_all + 2.0)
    scale = 1.0 / jnp.sqrt(2.0 * freq * (1.0 - freq))
    return ((rows.astype(jnp.float32) - 2.0 * freq) * scale).astype(jnp.bfloat16)


def on_device(dosages, allele_counts, partner):
    cohorts, blocks = lax.axis_size("cohort"), lax.axis_size("person")
    own = standard_rows(dosages[0], allele_counts[0], dosages.shape[1] * blocks)
    rounds = [
        functools.partial(one_round, round_number, cohorts, blocks)
        for round_number in range(1, cohorts)
    ]
    return lax.switch(partner[0] - 1, rounds, own)


def solution(mesh):
    placed = (P("cohort", "person", None), P("cohort", "person", None), P())
    return jax.shard_map(
        on_device,
        mesh=mesh,
        in_specs=placed,
        out_specs=P("cohort", "person", None),
        check_vma=False,
    )
```

time: 106 us -> 50.3 us (0.47); the launches traced: 105 us -> 50.1 us
  waiting for transfers between devices: 67.7 us -> 20.9 us
  between operations: 14.1 us -> 0.07 us
  starting transfers between devices: 4.91 us -> 14.9 us
  matrix products: 3.73 us -> 0 us
  other arithmetic: 3.08 us -> 1.24 us
  Pallas kernels: 0 us -> 1.76 us
    all_gather x1 -> x0, waiting for transfers between devices: 58.1 us -> none  [on_device(): lax.all_gather(partner_rows, 'person', axis=0, tiled=True)]
    ppermute x2 -> x7, waiting for transfers between devices: 9.52 us -> 20.9 us  [send(): return lax.ppermute(value, AXES, pairs)]
    ppermute x2 -> x7, starting transfers between devices: 4.91 us -> 14.9 us  [send(): return lax.ppermute(value, AXES, pairs)]
    dot_general x1 -> x0, matrix products: 3.73 us -> none  [cross_product(): lax.dot_general(left_rows, right_rows, (((1,), (1,)), ((), ())), preferre...]
    select_n x2 -> x0, other arithmetic: 1.93 us -> none  [on_device(): partner_rows = jnp.where(flag, moved, partner_rows)]
    pallas_call x0 -> x2, Pallas kernels: none -> 1.76 us  [the longest x1 1.15 us: multiply(): pl.pallas_call(functools.partial(multiply_kernel, half, math.sqrt(markers...]
    unnamed x0 -> x6, local copies, waits for them, and re-layouts: none -> 1.36 us
    dynamic_slice x1 -> x0, local copies, waits for them, and re-layouts: 1.24 us -> none  [on_device(): other_cohort = partner[own_cohort]]
  transfers between devices with their start and end apart: 3 -> 7, of which waited for: 2 -> 6; matrix products, arithmetic and copies ran while one was open for 1% -> 0% of each run, Pallas kernels for 0% -> 0%
where the time goes in v3:
time: 50.3 us; the launch traced here: 50.1 us
  waiting for transfers between devices  20.9 us (42%)
  starting transfers between devices  14.9 us (30%)
  blocking collectives  9.72 us (19%)
  Pallas kernels  1.76 us (3%)
  local copies, waits for them, and re-layouts  1.38 us (3%)
  other arithmetic  1.24 us (2%)
    ppermute x7, waiting for transfers between devices, send(): return lax.ppermute(value, AXES, pairs)  20.9 us
    ppermute x7, starting transfers between devices, send(): return lax.ppermute(value, AXES, pairs)  14.9 us
    psum x1, blocking collectives, standard_rows(): totals = lax.psum(counts, 'person')  9.72 us
    unnamed x6, local copies, waits for them, and re-layouts  1.36 us
    pallas_call x1, Pallas kernels, multiply(): pl.pallas_call(functools.partial(multiply_kernel, half, math.sqrt(markers...  1.15 us
    convert_element_type x1, other arithmetic, standard_rows(): ((rows.astype(jnp.float32) - 2.0 * freq) * scale).astype(jnp.bfloat16)  1.09 us
  transfers between devices with their start and end apart: 7, of which 6 were waited for; matrix products, arithmetic and copies ran while one was open for 0% of the time, Pallas kernels for 0%

profile of v3, /device:TPU:1, one launch (start us, length us, event | category | flops | bytes accessed | tf_op | source)
XLA Modules:
  0.0 50.1 jit_solution(8323078363226089168)
XLA Ops:
  0.0 0.0 copy-start.2
  0.0 0.0 copy-start.1
  0.0 0.7 %copy-done.2 = s32[4]{0:T(128)S(1)} copy-done((s32[4]{0:T(128)S(1)}, s32[4]{0:T(128)}, u32[]{:S(2)}) %copy-start.2) | copy-done | bytes 40
  0.7 0.0 copy-done.1
  0.7 9.7 %psum.7 = s32[1,1536]{1,0:T(1,128)S(1)} all-reduce(s32[1,1536]{1,0:T(1,128)S(1)} %bitcast.12), channel_id=1, replica_groups=mesh['cohort'=4,'person'=8] {'person'}, use_global_device_ids=true, to_apply=%region_0.0 | all-reduce | flops 1536 | bytes 12288 | tf_op jit(solution)/shard_map/psum | solution.py:173
  10.5 1.1 %fusion.1 = bf16[128,1536]{1,0:T(8,128)(2,1)S(1)} fusion(bf16[1,128,1536]{2,1,0:T(8,128)(2,1)} %param.6, f32[1536]{0:T(1024)S(1)} %get-tuple-element.20, f32[1536]{0:T(1024)S(1)} %get-tuple-element.19), kind=kLoop, calls=%fused_computation.11 | loop fusion | flops 786432 | bytes 798720 | tf_op jit(solution)/shard_map/convert_element_type | solution.py:176
  11.6 37.8 %conditional.1 = (bf16[1,128,1024]{2,1,0:T(8,128)(2,1)S(1)}) conditional(s32[]{:T(128)} %bitcast.6, bf16[128,1536]{1,0:T(8,128)(2,1)S(1)} %fusion.1, bf16[128,1536]{1,0:T(8,128)(2,1)S(1)} %fusion.1, bf16[128,1536]{1,0:T(8,128)(2,1)S(1)} %fusion.1), branch_computations={%region_1.0_spmd, %region_2.0_spmd, %region_3.0_spmd} | conditional | flops 131083 | bytes 8913278 | solution.py:186
  11.6 1.1 %collective-permute-start.7 = (bf16[128,1536]{1,0:T(8,128)(2,1)S(1)}, bf16[128,1536]{1,0:T(8,128)(2,1)S(1)}, u32[]{:S(2)}, u32[]{:S(2)}) collective-permute-start(bf16[128,1536]{1,0:T(8,128)(2,1)S(1)} %refs_0_.1), channel_id=1, source_target_pairs={{0,9},{20,0},{1,8},{21,1},{2,11},{22,2},{3,10},{23,3},{4,13},{16,4... | collective-permute-start | bytes 1179656 | tf_op jit(solution)/shard_map/cond/branch_1_fun/ppermute | solution.py:124
  12.7 4.0 %collective-permute-start.6 = (bf16[128,1536]{1,0:T(8,128)(2,1)S(1)}, bf16[128,1536]{1,0:T(8,128)(2,1)S(1)}, u32[]{:S(2)}, u32[]{:S(2)}) collective-permute-start(bf16[128,1536]{1,0:T(8,128)(2,1)S(1)} %refs_0_.1), channel_id=1, source_target_pairs={{0,2},{16,8},{1,3},{17,9},{2,0},{18,10},{3,1},{19,11},{4,6},{20,12... | collective-permute-start | bytes 1179656 | tf_op jit(solution)/shard_map/cond/branch_1_fun/ppermute | solution.py:124
  16.6 5.5 %collective-permute-done.7.refs_2_ = bf16[128,1536]{1,0:T(8,128)(2,1)S(1)} collective-permute-done((bf16[128,1536]{1,0:T(8,128)(2,1)S(1)}, bf16[128,1536]{1,0:T(8,128)(2,1)S(1)}, u32[]{:S(2)}, u32[]{:S(2)}) %collective-permute-start.7) | collective-permute-done | bytes 393248 | tf_op jit(solution)/shard_map/cond/branch_1_fun/ppermute | solution.py:124
  22.1 6.8 %collective-permute-start.9 = (bf16[128,1536]{1,0:T(8,128)(2,1)S(1)}, bf16[128,1536]{1,0:T(8,128)(2,1)S(1)}, u32[]{:S(2)}, u32[]{:S(2)}) collective-permute-start(bf16[128,1536]{1,0:T(8,128)(2,1)S(1)} %collective-permute-done.7.refs_2_), channel_id=1, source_target_pairs={{0,8},{8,0},{1,9},{9,1},{2,10},{10,2},{3,11},{11,3},{4,12},{12,4},... | collective-permute-start | bytes 1179656 | tf_op jit(solution)/shard_map/cond/branch_1_fun/ppermute | solution.py:124
  29.0 0.0 collective-permute-done.6.refs_1_
  29.0 0.0 collective-permute-start.8
  29.0 0.1 pad_add_fusion.1.role_ref
  29.1 1.3 %collective-permute-done.9.refs_4_ = bf16[128,1536]{1,0:T(8,128)(2,1)S(1)} collective-permute-done((bf16[128,1536]{1,0:T(8,128)(2,1)S(1)}, bf16[128,1536]{1,0:T(8,128)(2,1)S(1)}, u32[]{:S(2)}, u32[]{:S(2)}) %collective-permute-start.9) | collective-permute-done | bytes 393248 | tf_op jit(solution)/shard_map/cond/branch_1_fun/ppermute | solution.py:124
  30.3 5.9 %collective-permute-done.8.refs_3_ = bf16[128,1536]{1,0:T(8,128)(2,1)S(1)} collective-permute-done((bf16[128,1536]{1,0:T(8,128)(2,1)S(1)}, bf16[128,1536]{1,0:T(8,128)(2,1)S(1)}, u32[]{:S(2)}, u32[]{:S(2)}) %collective-permute-start.8) | collective-permute-done | bytes 393248 | tf_op jit(solution)/shard_map/cond/branch_1_fun/ppermute | solution.py:124
  36.2 1.2 %branch_1_fun.2 = (bf16[2,128,256]{2,1,0:T(8,128)(2,1)S(1)}, bf16[2,128,256]{2,1,0:T(8,128)(2,1)S(1)}) custom-call(s32[2]{0:T(128)S(1)} %pad_add_fusion.1.role_ref, bf16[128,1536]{1,0:T(8,128)(2,1)S(1)} %refs_0_.1, bf16[128,1536]{1,0:T(8,128)(2,1)S(1)} %collective-permute-done.6.refs_1_, bf16[128,1536]{1,0:T(8,128)(2,1)S(1)} %collective-permute-done.7.refs_2_, ...), custom_call_target="tpu_custom_call" | custom-call | tf_op jit(solution)/shard_map/cond/branch_1_fun/pallas_call | solution.py:67
  37.3 0.1 collective-permute-start.10
  37.4 1.9 %collective-permute-done.10 = bf16[2,128,256]{2,1,0:T(8,128)(2,1)S(1)} collective-permute-done((bf16[2,128,256]{2,1,0:T(8,128)(2,1)S(1)}, bf16[2,128,256]{2,1,0:T(8,128)(2,1)S(1)}, u32[]{:S(2)}, u32[]{:S(2)}) %collective-permute-start.10) | collective-permute-done | bytes 131104 | tf_op jit(solution)/shard_map/cond/branch_1_fun/ppermute | solution.py:124
  39.4 1.9 %collective-permute-start.11 = (bf16[2,128,256]{2,1,0:T(8,128)(2,1)S(1)}, bf16[2,128,256]{2,1,0:T(8,128)(2,1)S(1)}, u32[]{:S(2)}, u32[]{:S(2)}) collective-permute-start(bf16[2,128,256]{2,1,0:T(8,128)(2,1)S(1)} %pad_maximum_fusion.2), channel_id=1, source_target_pairs={{0,0},{8,16},{1,1},{9,17},{2,2},{10,18},{3,3},{11,19},{4,4},{12,20... | collective-permute-start | bytes 393224 | tf_op jit(solution)/shard_map/cond/branch_1_fun/ppermute | solution.py:124
  41.3 1.0 %collective-permute-start.12 = (bf16[2,128,256]{2,1,0:T(8,128)(2,1)S(1)}, bf16[2,128,256]{2,1,0:T(8,128)(2,1)S(1)}, u32[]{:S(2)}, u32[]{:S(2)}) collective-permute-start(bf16[2,128,256]{2,1,0:T(8,128)(2,1)S(1)} %pad_maximum_fusion.3), channel_id=1, source_target_pairs={{0,2},{8,20},{1,3},{9,21},{2,0},{10,22},{3,1},{11,23},{4,6},{12,16... | collective-permute-start | bytes 393224 | tf_op jit(solution)/shard_map/cond/branch_1_fun/ppermute | solution.py:124
  42.4 3.6 %collective-permute-done.11.refs_0_ = bf16[2,128,256]{2,1,0:T(8,128)(2,1)S(1)} collective-permute-done((bf16[2,128,256]{2,1,0:T(8,128)(2,1)S(1)}, bf16[2,128,256]{2,1,0:T(8,128)(2,1)S(1)}, u32[]{:S(2)}, u32[]{:S(2)}) %collective-permute-start.11) | collective-permute-done | bytes 131104 | tf_op jit(solution)/shard_map/cond/branch_1_fun/ppermute | solution.py:124
  46.0 2.8 %collective-permute-done.12.refs_1_ = bf16[2,128,256]{2,1,0:T(8,128)(2,1)S(1)} collective-permute-done((bf16[2,128,256]{2,1,0:T(8,128)(2,1)S(1)}, bf16[2,128,256]{2,1,0:T(8,128)(2,1)S(1)}, u32[]{:S(2)}, u32[]{:S(2)}) %collective-permute-start.12) | collective-permute-done | bytes 131104 | tf_op jit(solution)/shard_map/cond/branch_1_fun/ppermute | solution.py:124
  48.7 0.6 %branch_1_fun.3 = bf16[1,128,1024]{2,1,0:T(8,128)(2,1)S(1)} custom-call(s32[2]{0:T(128)S(1)} %pad_add_fusion.1.role_ref, bf16[2,128,256]{2,1,0:T(8,128)(2,1)S(1)} %collective-permute-done.11.refs_0_, bf16[2,128,256]{2,1,0:T(8,128)(2,1)S(1)} %collective-permute-done.12.refs_1_), custom_call_target="tpu_custom_call" | custom-call | tf_op jit(solution)/shard_map/cond/branch_1_fun/pallas_call | solution.py:103
  49.4 0.0 copy-start
  49.4 0.7 %copy-done = bf16[1,128,1024]{2,1,0:T(8,128)(2,1)} copy-done((bf16[1,128,1024]{2,1,0:T(8,128)(2,1)}, bf16[1,128,1024]{2,1,0:T(8,128)(2,1)S(1)}, u32[]{:S(2)}) %copy-start) | copy-done | bytes 262168
  (5 shorter events, 0.1 us)
Async XLA Ops:
  0.0 0.7 %copy-start.2 = (s32[4]{0:T(128)S(1)}, s32[4]{0:T(128)}, u32[]{:S(2)}) copy-start(s32[4]{0:T(128)} %param.8) | copy-start | bytes 52
  0.0 0.7 %copy-start.1 = (s32[1,1,1536]{2,1,0:T(1,128)S(1)}, s32[1,1,1536]{2,1,0:T(1,128)}, u32[]{:S(2)}) copy-start(s32[1,1,1536]{2,1,0:T(1,128)} %param.7) | copy-start | bytes 18436
  11.6 10.5 %collective-permute-start.7 = (bf16[128,1536]{1,0:T(8,128)(2,1)S(1)}, bf16[128,1536]{1,0:T(8,128)(2,1)S(1)}, u32[]{:S(2)}, u32[]{:S(2)}) collective-permute-start(bf16[128,1536]{1,0:T(8,128)(2,1)S(1)} %refs_0_.1), channel_id=1, source_target_pairs={{0,9},{20,0},{1,8},{21,1},{2,11},{22,2},{3,10},{23,3},{4,13},{16,4... | collective-permute-start | bytes 1179656 | tf_op jit(solution)/shard_map/cond/branch_1_fun/ppermute | solution.py:124
  12.7 16.3 %collective-permute-start.6 = (bf16[128,1536]{1,0:T(8,128)(2,1)S(1)}, bf16[128,1536]{1,0:T(8,128)(2,1)S(1)}, u32[]{:S(2)}, u32[]{:S(2)}) collective-permute-start(bf16[128,1536]{1,0:T(8,128)(2,1)S(1)} %refs_0_.1), channel_id=1, source_target_pairs={{0,2},{16,8},{1,3},{17,9},{2,0},{18,10},{3,1},{19,11},{4,6},{20,12... | collective-permute-start | bytes 1179656 | tf_op jit(solution)/shard_map/cond/branch_1_fun/ppermute | solution.py:124
  22.1 8.2 %collective-permute-start.9 = (bf16[128,1536]{1,0:T(8,128)(2,1)S(1)}, bf16[128,1536]{1,0:T(8,128)(2,1)S(1)}, u32[]{:S(2)}, u32[]{:S(2)}) collective-permute-start(bf16[128,1536]{1,0:T(8,128)(2,1)S(1)} %collective-permute-done.7.refs_2_), channel_id=1, source_target_pairs={{0,8},{8,0},{1,9},{9,1},{2,10},{10,2},{3,11},{11,3},{4,12},{12,4},... | collective-permute-start | bytes 1179656 | tf_op jit(solution)/shard_map/cond/branch_1_fun/ppermute | solution.py:124
  29.0 7.2 %collective-permute-start.8 = (bf16[128,1536]{1,0:T(8,128)(2,1)S(1)}, bf16[128,1536]{1,0:T(8,128)(2,1)S(1)}, u32[]{:S(2)}, u32[]{:S(2)}) collective-permute-start(bf16[128,1536]{1,0:T(8,128)(2,1)S(1)} %collective-permute-done.6.refs_1_), channel_id=1, source_target_pairs={{0,9},{8,0},{1,8},{9,1},{2,11},{10,2},{3,10},{11,3},{4,13},{12,4},... | collective-permute-start | bytes 1179656 | tf_op jit(solution)/shard_map/cond/branch_1_fun/ppermute | solution.py:124
  37.3 2.0 %collective-permute-start.10 = (bf16[2,128,256]{2,1,0:T(8,128)(2,1)S(1)}, bf16[2,128,256]{2,1,0:T(8,128)(2,1)S(1)}, u32[]{:S(2)}, u32[]{:S(2)}) collective-permute-start(bf16[2,128,256]{2,1,0:T(8,128)(2,1)S(1)} %get-tuple-element.15), channel_id=1, source_target_pairs={{8,1},{0,8},{9,0},{1,9},{10,3},{2,10},{11,2},{3,11},{12,5},{4,12},... | collective-permute-start | bytes 393224 | tf_op jit(solution)/shard_map/cond/branch_1_fun/ppermute | solution.py:124
  39.4 6.6 %collective-permute-start.11 = (bf16[2,128,256]{2,1,0:T(8,128)(2,1)S(1)}, bf16[2,128,256]{2,1,0:T(8,128)(2,1)S(1)}, u32[]{:S(2)}, u32[]{:S(2)}) collective-permute-start(bf16[2,128,256]{2,1,0:T(8,128)(2,1)S(1)} %pad_maximum_fusion.2), channel_id=1, source_target_pairs={{0,0},{8,16},{1,1},{9,17},{2,2},{10,18},{3,3},{11,19},{4,4},{12,20... | collective-permute-start | bytes 393224 | tf_op jit(solution)/shard_map/cond/branch_1_fun/ppermute | solution.py:124
  41.3 7.4 %collective-permute-start.12 = (bf16[2,128,256]{2,1,0:T(8,128)(2,1)S(1)}, bf16[2,128,256]{2,1,0:T(8,128)(2,1)S(1)}, u32[]{:S(2)}, u32[]{:S(2)}) collective-permute-start(bf16[2,128,256]{2,1,0:T(8,128)(2,1)S(1)} %pad_maximum_fusion.3), channel_id=1, source_target_pairs={{0,2},{8,20},{1,3},{9,21},{2,0},{10,22},{3,1},{11,23},{4,6},{12,16... | collective-permute-start | bytes 393224 | tf_op jit(solution)/shard_map/cond/branch_1_fun/ppermute | solution.py:124
  49.4 0.7 %copy-start = (bf16[1,128,1024]{2,1,0:T(8,128)(2,1)}, bf16[1,128,1024]{2,1,0:T(8,128)(2,1)S(1)}, u32[]{:S(2)}) copy-start(bf16[1,128,1024]{2,1,0:T(8,128)(2,1)S(1)} %get-tuple-element.68) | copy-start | bytes 786436

commit v4 on v3

v4 whole, which is shorter than its diff:
```python
import functools
import math

import jax
import jax.numpy as jnp
from jax import lax
from jax.experimental import pallas as pl
from jax.experimental.pallas import tpu as pltpu
from jax.sharding import PartitionSpec as P

AXES = ("cohort", "person")
VMEM_BYTES = 48 * 1024 * 1024


def left_cohorts(cohorts, round_number):
    if round_number == 1:
        return [c for c in range(cohorts) if c & 1 == 0]
    top = 1 << (round_number.bit_length() - 1)
    return [
        c
        for c in range(cohorts)
        if (c & top == 0 and c & 1 == 0) or (c & top and (c ^ round_number ^ 1) & 1 == 0)
    ]


def half_size(blocks):
    return 1 << (blocks.bit_length() // 2 - 1)


def far_step(half, m):
    return 2 * half * m + half * (m & 1)


def flipped(half, place):
    low, high = half.bit_length() - 1, half.bit_length()
    return ((place >> low) ^ (place >> high)) & 1


def standard_kernel(people_all, *refs):
    counts, rows_ref, out_ref = refs[:-2], refs[-2], refs[-1]
    totals = counts[0][...]
    for part in counts[1:]:
        totals = totals + part[...]
    freq = (totals.astype(jnp.float32) + 1.0) / (2.0 * people_all + 2.0)
    scale = 1.0 / jnp.sqrt(2.0 * freq * (1.0 - freq))
    rows = rows_ref[...].astype(jnp.float32)
    out_ref[...] = ((rows - 2.0 * freq) * scale).astype(jnp.bfloat16)


def standard_rows(rows, counts, people_all):
    vmem = pl.BlockSpec(memory_space=pltpu.VMEM)
    return pl.pallas_call(
        functools.partial(standard_kernel, people_all),
        out_shape=jax.ShapeDtypeStruct(rows.shape, jnp.bfloat16),
        in_specs=[vmem] * (len(counts) + 1),
        out_specs=vmem,
        compiler_params=pltpu.CompilerParams(vmem_limit_bytes=VMEM_BYTES),
    )(*counts, rows)


def multiply_kernel(half, root, role_ref, *refs):
    shards, send_ref, keep_ref = refs[: 3 * half], refs[3 * half : 4 * half], refs[4 * half :]
    across = shards[:half]
    fetched, passed = shards[half : 2 * half], shards[2 * half :]
    rows = across[0].shape[0]

    def product(first, second):
        dims = (((1,), (1,)), ((), ()))
        out = lax.dot_general(first, second, dims, preferred_element_type=jnp.float32)
        return (out / root).astype(jnp.bfloat16)

    def store(lefts, rights, left_ref, right_ref):
        left_all = jnp.concatenate([part[...] for part in lefts], axis=0)
        right_all = jnp.concatenate([part[...] for part in rights], axis=0)
        by_left = product(left_all, right_all)
        by_right = product(right_all, left_all)
        for t in range(half):
            left_ref[t][...] = by_left[t * rows : (t + 1) * rows]
            right_ref[t][...] = by_right[t * rows : (t + 1) * rows]

    @pl.when(role_ref[0] == 1)
    def _():
        store(across, fetched, keep_ref, send_ref)

    @pl.when(role_ref[0] == 0)
    def _():
        store(fetched, passed, send_ref, keep_ref)


def multiply(role, half, across, fetched, passed):
    rows, markers = across[0].shape
    shards = [*across, *fetched, *passed]
    vmem = pl.BlockSpec(memory_space=pltpu.VMEM)
    block = jax.ShapeDtypeStruct((rows, half * rows), jnp.bfloat16)
    outs = pl.pallas_call(
        functools.partial(multiply_kernel, half, math.sqrt(markers)),
        out_shape=[block] * (2 * half),
        in_specs=[pl.BlockSpec(memory_space=pltpu.SMEM)] + [vmem] * len(shards),
        out_specs=[vmem] * (2 * half),
        compiler_params=pltpu.CompilerParams(vmem_limit_bytes=VMEM_BYTES),
    )(role, *shards)
    return outs[:half], outs[half:]


def place_kernel(half, role_ref, *refs):
    sent, kept, out_ref = refs[:half], refs[half:-1], refs[-1]
    rows = out_ref.shape[1]
    place = role_ref[1]
    flip = flipped(half, place)

    def put(block, value):
        out_ref[0, :, pl.ds(pl.multiple_of(block * rows, rows), rows)] = value

    @pl.when(role_ref[0] == 1)
    def _():
        for t in range(half):
            for part, chip in ((kept[t], place ^ 2 * t), (sent[t], place ^ 2 * t + 1)):
                turn = flipped(half, chip)
                for m in range(half):
                    put(chip ^ far_step(half, m ^ turn), part[:, m * rows : (m + 1) * rows])

    @pl.when(role_ref[0] == 0)
    def _():
        for t in range(half):
            chip = place ^ far_step(half, t ^ flip)
            for d in range(half):
                put(chip ^ 2 * d, sent[t][:, d * rows : (d + 1) * rows])
                put(chip ^ 2 * d + 1, kept[t][:, d * rows : (d + 1) * rows])


def place_blocks(role, half, sent, kept):
    rows = sent[0].shape[0]
    vmem = pl.BlockSpec(memory_space=pltpu.VMEM)
    return pl.pallas_call(
        functools.partial(place_kernel, half),
        out_shape=jax.ShapeDtypeStruct((1, rows, 2 * half * half * rows), jnp.bfloat16),
        in_specs=[pl.BlockSpec(memory_space=pltpu.SMEM)] + [vmem] * (2 * half),
        out_specs=vmem,
        compiler_params=pltpu.CompilerParams(vmem_limit_bytes=VMEM_BYTES),
    )(role, *sent, *kept)


def one_round(round_number, cohorts, blocks, own):
    half = half_size(blocks)
    left = left_cohorts(cohorts, round_number)

    def send(value, *legs):
        pairs = []
        for c in left:
            for i in range(blocks):
                for leg in legs:
                    (c0, i0), (c1, i1) = leg(c, i)
                    pairs.append((c0 * blocks + i0, c1 * blocks + i1))
        return lax.ppermute(value, AXES, pairs)

    def right(i, t):
        return i ^ far_step(half, t ^ flipped(half, i))

    def left_to_left(d):
        return lambda c, i: ((c, i), (c, i ^ d))

    def left_to_mate(d):
        return lambda c, i: ((c, i), (c ^ 1, i ^ d))

    def mate_to_left(d):
        return lambda c, i: ((c ^ 1, i), (c, i ^ d))

    def mate_to_mate(c, i):
        return (c ^ 1, i), (c ^ 1, i)

    def owner_to_left(t):
        return lambda c, i: ((c ^ round_number, right(i, t)), (c, i))

    def left_to_owner(t):
        return lambda c, i: ((c, i), (c ^ round_number, right(i, t)))

    def mate_to_owner(t):
        return lambda c, i: ((c ^ 1, i), (c ^ round_number, right(i, t)))

    cohort = lax.axis_index("cohort")
    is_left = functools.reduce(jnp.logical_or, [cohort == c for c in left])
    role = jnp.stack([is_left.astype(jnp.int32), lax.axis_index("person")])

    across = [own] + [send(own, left_to_left(2 * t), mate_to_mate) for t in range(1, half)]
    fetched = [send(across[t], left_to_mate(1), owner_to_left(t)) for t in range(half)]
    passed = [send(fetched[t], left_to_mate(0), mate_to_left(0)) for t in range(half)]
    sent, kept = multiply(role, half, across, fetched, passed)
    sent, kept = list(sent), list(kept)
    for t in reversed(range(half)):
        sent[t] = send(sent[t], mate_to_left(2 * t + 1), left_to_owner(t))
        kept[t] = send(kept[t], left_to_left(2 * t), mate_to_owner(t))
    return place_blocks(role, half, sent, kept)


def on_device(dosages, allele_counts, partner):
    cohorts, blocks = lax.axis_size("cohort"), lax.axis_size("person")
    half = half_size(blocks)

    def swap(value, step):
        return lax.ppermute(value, "person", [(i, i ^ step) for i in range(blocks)])

    near = allele_counts[0]
    for step in range(1, 2 * half):
        near = near + swap(allele_counts[0], step)
    counts = [near] + [swap(near, far_step(half, m)) for m in range(1, half)]
    own = standard_rows(dosages[0], counts, dosages.shape[1] * blocks)
    rounds = [
        functools.partial(one_round, round_number, cohorts, blocks)
        for round_number in range(1, cohorts)
    ]
    return lax.switch(partner[0] - 1, rounds, own)


def solution(mesh):
    placed = (P("cohort", "person", None), P("cohort", "person", None), P())
    return jax.shard_map(
        on_device,
        mesh=mesh,
        in_specs=placed,
        out_specs=P("cohort", "person", None),
        check_vma=False,
    )
```

time: 50.3 us -> 49.6 us (0.986)
  starting transfers between devices: 14.9 us -> 32.1 us
  blocking collectives: 9.72 us -> 0 us
  waiting for transfers between devices: 20.9 us -> 12.7 us
    ppermute x7 -> x9, waiting for transfers between devices: 20.9 us -> 9.12 us  [send(): return lax.ppermute(value, AXES, pairs)]
    ppermute x7 -> x9, starting transfers between devices: 14.9 us -> 25 us  [send(): return lax.ppermute(value, AXES, pairs)]
    psum x1 -> x0, blocking collectives: 9.72 us -> none  [standard_rows(): totals = lax.psum(counts, 'person')]
    ppermute x0 -> x4, starting transfers between devices: none -> 7.05 us  [swap(): return lax.ppermute(value, 'person', [(i, i ^ step) for i in range(blocks)])]
    ppermute x0 -> x4, waiting for transfers between devices: none -> 3.54 us  [swap(): return lax.ppermute(value, 'person', [(i, i ^ step) for i in range(blocks)])]
    convert_element_type x1 -> x0, other arithmetic: 1.09 us -> none  [standard_rows(): ((rows.astype(jnp.float32) - 2.0 * freq) * scale).astype(jnp.bfloat16)]
    add x0 -> x1, other arithmetic: none -> 0.7 us  [on_device(): near = near + swap(allele_counts[0], step)]
  transfers between devices with their start and end apart: 7 -> 13, of which waited for: 6 -> 7; matrix products, arithmetic and copies ran while one was open for 0% -> 0% of each run, Pallas kernels for 0% -> 0%
where the time goes in v4:
time: 49.6 us; the launch traced here: 49.2 us
  starting transfers between devices  32.1 us (65%)
  waiting for transfers between devices  12.7 us (26%)
  Pallas kernels  1.86 us (4%)
  local copies, waits for them, and re-layouts  1.7 us (3%)
  other arithmetic  0.78 us (2%)
    ppermute x9, starting transfers between devices, send(): return lax.ppermute(value, AXES, pairs)  25 us
    ppermute x9, waiting for transfers between devices, send(): return lax.ppermute(value, AXES, pairs)  9.12 us
    ppermute x4, starting transfers between devices, swap(): return lax.ppermute(value, 'person', [(i, i ^ step) for i in range(blocks)])  7.05 us
    ppermute x4, waiting for transfers between devices, swap(): return lax.ppermute(value, 'person', [(i, i ^ step) for i in range(blocks)])  3.54 us
    unnamed x6, local copies, waits for them, and re-layouts  1.7 us
    pallas_call x1, Pallas kernels, multiply(): pl.pallas_call(functools.partial(multiply_kernel, half, math.sqrt(markers...  1.15 us
  transfers between devices with their start and end apart: 13, of which 7 were waited for; matrix products, arithmetic and copies ran while one was open for 0% of the time, Pallas kernels for 0%

profile of v4, /device:TPU:1, one launch (start us, length us, event | category | flops | bytes accessed | tf_op | source)
XLA Modules:
  0.0 49.2 jit_solution(18229182515212283493)
XLA Ops:
  0.0 2.1 %collective-permute-start.28 = (s32[1,1536]{1,0:T(1,128)}, s32[1,1536]{1,0:T(1,128)S(1)}, u32[]{:S(2)}, u32[]{:S(2)}) collective-permute-start(s32[1,1536]{1,0:T(1,128)} %bitcast.12), channel_id=1, source_target_pairs={{0,2},{1,3},{2,0},{3,1},{4,6},{5,7},{6,4},{7,5},{8,10},{9,11},{10,... | collective-permute-start | bytes 18440 | tf_op jit(solution)/shard_map/ppermute | solution.py:200
  2.1 1.1 %collective-permute-start.29 = (s32[1,1536]{1,0:T(1,128)}, s32[1,1536]{1,0:T(1,128)S(1)}, u32[]{:S(2)}, u32[]{:S(2)}) collective-permute-start(s32[1,1536]{1,0:T(1,128)} %bitcast.13), channel_id=1, source_target_pairs={{0,3},{1,2},{2,1},{3,0},{4,7},{5,6},{6,5},{7,4},{8,11},{9,10},{10,... | collective-permute-start | bytes 18440 | tf_op jit(solution)/shard_map/ppermute | solution.py:200
  3.3 0.1 collective-permute-start.27
  3.4 0.0 collective-permute-done.28
  3.4 2.3 %collective-permute-done.29 = s32[1,1536]{1,0:T(1,128)S(1)} collective-permute-done((s32[1,1536]{1,0:T(1,128)}, s32[1,1536]{1,0:T(1,128)S(1)}, u32[]{:S(2)}, u32[]{:S(2)}) %collective-permute-start.29) | collective-permute-done | bytes 6176 | tf_op jit(solution)/shard_map/ppermute | solution.py:200
  5.7 0.2 collective-permute-done.27
  5.9 0.7 %add_add_fusion.refs_0_ = s32[1,1536]{1,0:T(1,128)S(1)} fusion(s32[1,1536]{1,0:T(1,128)S(1)} %collective-permute-done.29, s32[1,1536]{1,0:T(1,128)S(1)} %collective-permute-done.28, s32[1,1536]{1,0:T(1,128)S(1)} %collective-permute-done.27, s32[1,1,1536]{2,1,0:T(1,128)} %param.7), kind=kLoop, calls=%fused_computation.3 | loop fusion | flops 4608 | bytes 30720 | tf_op jit(solution)/shard_map/add | solution.py:204
  6.7 0.0 copy-start.2
  6.7 3.7 %collective-permute-start.30 = (s32[1,1536]{1,0:T(1,128)S(1)}, s32[1,1536]{1,0:T(1,128)S(1)}, u32[]{:S(2)}, u32[]{:S(2)}) collective-permute-start(s32[1,1536]{1,0:T(1,128)S(1)} %add_add_fusion.refs_0_), channel_id=1, source_target_pairs={{0,6},{1,7},{2,4},{3,5},{4,2},{5,3},{6,0},{7,1},{8,14},{9,15},{10,... | collective-permute-start | bytes 18440 | tf_op jit(solution)/shard_map/ppermute | solution.py:200
  10.3 0.0 copy-done.2
  10.4 1.0 %collective-permute-done.30.refs_1_ = s32[1,1536]{1,0:T(1,128)S(1)} collective-permute-done((s32[1,1536]{1,0:T(1,128)S(1)}, s32[1,1536]{1,0:T(1,128)S(1)}, u32[]{:S(2)}, u32[]{:S(2)}) %collective-permute-start.30) | collective-permute-done | bytes 6176 | tf_op jit(solution)/shard_map/ppermute | solution.py:200
  11.4 0.0 copy-start
  11.4 1.0 %copy-done = bf16[1,128,1536]{2,1,0:T(8,128)(2,1)S(1)} copy-done((bf16[1,128,1536]{2,1,0:T(8,128)(2,1)S(1)}, bf16[1,128,1536]{2,1,0:T(8,128)(2,1)}, u32[]{:S(2)}) %copy-start) | copy-done | bytes 393240
  12.4 0.1 shard_map.40
  12.5 36.1 %conditional.1 = (bf16[1,128,1024]{2,1,0:T(8,128)(2,1)S(1)}) conditional(s32[]{:T(128)} %bitcast.6, bf16[128,1536]{1,0:T(8,128)(2,1)S(1)} %shard_map.40, bf16[128,1536]{1,0:T(8,128)(2,1)S(1)} %shard_map.40, bf16[128,1536]{1,0:T(8,128)(2,1)S(1)} %shard_map.40), branch_computations={%region_0.0_spmd, %region_1.0_spmd, %region_2.0_spmd} | conditional | flops 11 | bytes 8913358 | solution.py:211
  12.5 0.7 %collective-permute-start.18 = (bf16[128,1536]{1,0:T(8,128)(2,1)S(1)}, bf16[128,1536]{1,0:T(8,128)(2,1)S(1)}, u32[]{:S(2)}, u32[]{:S(2)}) collective-permute-start(bf16[128,1536]{1,0:T(8,128)(2,1)S(1)} %refs_0_.2), channel_id=1, source_target_pairs={{0,2},{8,8},{1,3},{9,9},{2,0},{10,10},{3,1},{11,11},{4,6},{12,12},... | collective-permute-start | bytes 1179656 | tf_op jit(solution)/shard_map/cond/branch_2_fun/ppermute | solution.py:154
  13.2 5.6 %collective-permute-start.19 = (bf16[128,1536]{1,0:T(8,128)(2,1)S(1)}, bf16[128,1536]{1,0:T(8,128)(2,1)S(1)}, u32[]{:S(2)}, u32[]{:S(2)}) collective-permute-start(bf16[128,1536]{1,0:T(8,128)(2,1)S(1)} %refs_0_.2), channel_id=1, source_target_pairs={{0,9},{24,0},{1,8},{25,1},{2,11},{28,2},{3,10},{29,3},{4,13},{26,4... | collective-permute-start | bytes 1179656 | tf_op jit(solution)/shard_map/cond/branch_2_fun/ppermute | solution.py:154
  18.8 0.0 collective-permute-done.18.refs_1_
  18.8 10.7 %collective-permute-start.20 = (bf16[128,1536]{1,0:T(8,128)(2,1)S(1)}, bf16[128,1536]{1,0:T(8,128)(2,1)S(1)}, u32[]{:S(2)}, u32[]{:S(2)}) collective-permute-start(bf16[128,1536]{1,0:T(8,128)(2,1)S(1)} %collective-permute-done.18.refs_1_), channel_id=1, source_target_pairs={{0,9},{30,0},{1,8},{31,1},{2,11},{26,2},{3,10},{27,3},{4,13},{28,4... | collective-permute-start | bytes 1179656 | tf_op jit(solution)/shard_map/cond/branch_2_fun/ppermute | solution.py:154
  29.5 0.0 collective-permute-done.19.refs_2_
  29.5 0.0 collective-permute-start.21
  29.5 4.7 %collective-permute-done.20.refs_3_ = bf16[128,1536]{1,0:T(8,128)(2,1)S(1)} collective-permute-done((bf16[128,1536]{1,0:T(8,128)(2,1)S(1)}, bf16[128,1536]{1,0:T(8,128)(2,1)S(1)}, u32[]{:S(2)}, u32[]{:S(2)}) %collective-permute-start.20) | collective-permute-done | bytes 393248 | tf_op jit(solution)/shard_map/cond/branch_2_fun/ppermute | solution.py:154
  34.2 1.0 %collective-permute-start.22 = (bf16[128,1536]{1,0:T(8,128)(2,1)S(1)}, bf16[128,1536]{1,0:T(8,128)(2,1)S(1)}, u32[]{:S(2)}, u32[]{:S(2)}) collective-permute-start(bf16[128,1536]{1,0:T(8,128)(2,1)S(1)} %collective-permute-done.20.refs_3_), channel_id=1, source_target_pairs={{0,8},{8,0},{1,9},{9,1},{2,10},{10,2},{3,11},{11,3},{4,12},{12,4},... | collective-permute-start | bytes 1179656 | tf_op jit(solution)/shard_map/cond/branch_2_fun/ppermute | solution.py:154
  35.2 0.1 pad_add_fusion.2.role_ref
  35.3 0.0 collective-permute-done.21.refs_4_
  35.3 1.3 %collective-permute-done.22.refs_5_ = bf16[128,1536]{1,0:T(8,128)(2,1)S(1)} collective-permute-done((bf16[128,1536]{1,0:T(8,128)(2,1)S(1)}, bf16[128,1536]{1,0:T(8,128)(2,1)S(1)}, u32[]{:S(2)}, u32[]{:S(2)}) %collective-permute-start.22) | collective-permute-done | bytes 393248 | tf_op jit(solution)/shard_map/cond/branch_2_fun/ppermute | solution.py:154
  36.6 1.1 %branch_2_fun.2 = (bf16[128,256]{1,0:T(8,128)(2,1)S(1)}, bf16[128,256]{1,0:T(8,128)(2,1)S(1)}, bf16[128,256]{1,0:T(8,128)(2,1)S(1)}, bf16[128,256]{1,0:T(8,128)(2,1)S(1)}) custom-call(s32[2]{0:T(128)S(1)} %pad_add_fusion.2.role_ref, bf16[128,1536]{1,0:T(8,128)(2,1)S(1)} %refs_0_.2, bf16[128,1536]{1,0:T(8,128)(2,1)S(1)} %collective-permute-done.18.refs_1_, ...), custom_call_target="tpu_custom_call" | custom-call | tf_op jit(solution)/shard_map/cond/branch_2_fun/pallas_call | solution.py:95
  37.8 1.1 %collective-permute-start.23 = (bf16[128,256]{1,0:T(8,128)(2,1)S(1)}, bf16[128,256]{1,0:T(8,128)(2,1)S(1)}, u32[]{:S(2)}, u32[]{:S(2)}) collective-permute-start(bf16[128,256]{1,0:T(8,128)(2,1)S(1)} %get-tuple-element.20), channel_id=1, source_target_pairs={{8,1},{0,24},{9,0},{1,25},{10,3},{2,28},{11,2},{3,29},{12,5},{4,26... | collective-permute-start | bytes 196616 | tf_op jit(solution)/shard_map/cond/branch_2_fun/ppermute | solution.py:154
  38.8 0.0 collective-permute-start.24
  38.8 3.1 %collective-permute-start.25 = (bf16[128,256]{1,0:T(8,128)(2,1)S(1)}, bf16[128,256]{1,0:T(8,128)(2,1)S(1)}, u32[]{:S(2)}, u32[]{:S(2)}) collective-permute-start(bf16[128,256]{1,0:T(8,128)(2,1)S(1)} %get-tuple-element.22), channel_id=1, source_target_pairs={{0,0},{8,24},{1,1},{9,25},{2,2},{10,28},{3,3},{11,29},{4,4},{12,26... | collective-permute-start | bytes 196616 | tf_op jit(solution)/shard_map/cond/branch_2_fun/ppermute | solution.py:154
  41.9 2.9 %collective-permute-start.26 = (bf16[128,256]{1,0:T(8,128)(2,1)S(1)}, bf16[128,256]{1,0:T(8,128)(2,1)S(1)}, u32[]{:S(2)}, u32[]{:S(2)}) collective-permute-start(bf16[128,256]{1,0:T(8,128)(2,1)S(1)} %get-tuple-element.23), channel_id=1, source_target_pairs={{0,2},{8,30},{1,3},{9,31},{2,0},{10,26},{3,1},{11,27},{4,6},{12,28... | collective-permute-start | bytes 196616 | tf_op jit(solution)/shard_map/cond/branch_2_fun/ppermute | solution.py:154
  44.8 0.0 collective-permute-done.23.refs_0_
  44.8 0.4 collective-permute-done.24.refs_1_
  45.2 0.0 collective-permute-done.25.refs_2_
  45.2 2.7 %collective-permute-done.26.refs_3_ = bf16[128,256]{1,0:T(8,128)(2,1)S(1)} collective-permute-done((bf16[128,256]{1,0:T(8,128)(2,1)S(1)}, bf16[128,256]{1,0:T(8,128)(2,1)S(1)}, u32[]{:S(2)}, u32[]{:S(2)}) %collective-permute-start.26) | collective-permute-done | bytes 65568 | tf_op jit(solution)/shard_map/cond/branch_2_fun/ppermute | solution.py:154
  47.9 0.6 %branch_2_fun.3 = bf16[1,128,1024]{2,1,0:T(8,128)(2,1)S(1)} custom-call(s32[2]{0:T(128)S(1)} %pad_add_fusion.2.role_ref, bf16[128,256]{1,0:T(8,128)(2,1)S(1)} %collective-permute-done.23.refs_0_, bf16[128,256]{1,0:T(8,128)(2,1)S(1)} %collective-permute-done.24.refs_1_, bf16[128,256]{1,0:T(8,128)(2,1)S(1)} %collective-permute-done.25.refs_2_, ...), custom_call_target="tpu_custom_call" | custom-call | tf_op jit(solution)/shard_map/cond/branch_2_fun/pallas_call | solution.py:134
  48.5 0.0 copy-start.1
  48.5 0.7 %copy-done.1 = bf16[1,128,1024]{2,1,0:T(8,128)(2,1)} copy-done((bf16[1,128,1024]{2,1,0:T(8,128)(2,1)}, bf16[1,128,1024]{2,1,0:T(8,128)(2,1)S(1)}, u32[]{:S(2)}) %copy-start.1) | copy-done | bytes 262168
Async XLA Ops:
  0.0 3.4 %collective-permute-start.28 = (s32[1,1536]{1,0:T(1,128)}, s32[1,1536]{1,0:T(1,128)S(1)}, u32[]{:S(2)}, u32[]{:S(2)}) collective-permute-start(s32[1,1536]{1,0:T(1,128)} %bitcast.12), channel_id=1, source_target_pairs={{0,2},{1,3},{2,0},{3,1},{4,6},{5,7},{6,4},{7,5},{8,10},{9,11},{10,... | collective-permute-start | bytes 18440 | tf_op jit(solution)/shard_map/ppermute | solution.py:200
  2.1 3.6 %collective-permute-start.29 = (s32[1,1536]{1,0:T(1,128)}, s32[1,1536]{1,0:T(1,128)S(1)}, u32[]{:S(2)}, u32[]{:S(2)}) collective-permute-start(s32[1,1536]{1,0:T(1,128)} %bitcast.13), channel_id=1, source_target_pairs={{0,3},{1,2},{2,1},{3,0},{4,7},{5,6},{6,5},{7,4},{8,11},{9,10},{10,... | collective-permute-start | bytes 18440 | tf_op jit(solution)/shard_map/ppermute | solution.py:200
  3.3 2.7 %collective-permute-start.27 = (s32[1,1536]{1,0:T(1,128)}, s32[1,1536]{1,0:T(1,128)S(1)}, u32[]{:S(2)}, u32[]{:S(2)}) collective-permute-start(s32[1,1536]{1,0:T(1,128)} %bitcast.14), channel_id=1, source_target_pairs={{0,1},{1,0},{2,3},{3,2},{4,5},{5,4},{6,7},{7,6},{8,9},{9,8},{10,11... | collective-permute-start | bytes 18440 | tf_op jit(solution)/shard_map/ppermute | solution.py:200
  6.7 3.7 %copy-start.2 = (s32[4]{0:T(128)S(1)}, s32[4]{0:T(128)}, u32[]{:S(2)}) copy-start(s32[4]{0:T(128)} %param.8) | copy-start | bytes 52
  6.7 4.7 %collective-permute-start.30 = (s32[1,1536]{1,0:T(1,128)S(1)}, s32[1,1536]{1,0:T(1,128)S(1)}, u32[]{:S(2)}, u32[]{:S(2)}) collective-permute-start(s32[1,1536]{1,0:T(1,128)S(1)} %add_add_fusion.refs_0_), channel_id=1, source_target_pairs={{0,6},{1,7},{2,4},{3,5},{4,2},{5,3},{6,0},{7,1},{8,14},{9,15},{10,... | collective-permute-start | bytes 18440 | tf_op jit(solution)/shard_map/ppermute | solution.py:200
  11.4 1.0 %copy-start = (bf16[1,128,1536]{2,1,0:T(8,128)(2,1)S(1)}, bf16[1,128,1536]{2,1,0:T(8,128)(2,1)}, u32[]{:S(2)}) copy-start(bf16[1,128,1536]{2,1,0:T(8,128)(2,1)} %param.6) | copy-start | bytes 1179652
  12.5 6.3 %collective-permute-start.18 = (bf16[128,1536]{1,0:T(8,128)(2,1)S(1)}, bf16[128,1536]{1,0:T(8,128)(2,1)S(1)}, u32[]{:S(2)}, u32[]{:S(2)}) collective-permute-start(bf16[128,1536]{1,0:T(8,128)(2,1)S(1)} %refs_0_.2), channel_id=1, source_target_pairs={{0,2},{8,8},{1,3},{9,9},{2,0},{10,10},{3,1},{11,11},{4,6},{12,12},... | collective-permute-start | bytes 1179656 | tf_op jit(solution)/shard_map/cond/branch_2_fun/ppermute | solution.py:154
  13.2 16.3 %collective-permute-start.19 = (bf16[128,1536]{1,0:T(8,128)(2,1)S(1)}, bf16[128,1536]{1,0:T(8,128)(2,1)S(1)}, u32[]{:S(2)}, u32[]{:S(2)}) collective-permute-start(bf16[128,1536]{1,0:T(8,128)(2,1)S(1)} %refs_0_.2), channel_id=1, source_target_pairs={{0,9},{24,0},{1,8},{25,1},{2,11},{28,2},{3,10},{29,3},{4,13},{26,4... | collective-permute-start | bytes 1179656 | tf_op jit(solution)/shard_map/cond/branch_2_fun/ppermute | solution.py:154
  18.8 15.4 %collective-permute-start.20 = (bf16[128,1536]{1,0:T(8,128)(2,1)S(1)}, bf16[128,1536]{1,0:T(8,128)(2,1)S(1)}, u32[]{:S(2)}, u32[]{:S(2)}) collective-permute-start(bf16[128,1536]{1,0:T(8,128)(2,1)S(1)} %collective-permute-done.18.refs_1_), channel_id=1, source_target_pairs={{0,9},{30,0},{1,8},{31,1},{2,11},{26,2},{3,10},{27,3},{4,13},{28,4... | collective-permute-start | bytes 1179656 | tf_op jit(solution)/shard_map/cond/branch_2_fun/ppermute | solution.py:154
  29.5 5.8 %collective-permute-start.21 = (bf16[128,1536]{1,0:T(8,128)(2,1)S(1)}, bf16[128,1536]{1,0:T(8,128)(2,1)S(1)}, u32[]{:S(2)}, u32[]{:S(2)}) collective-permute-start(bf16[128,1536]{1,0:T(8,128)(2,1)S(1)} %collective-permute-done.19.refs_2_), channel_id=1, source_target_pairs={{0,8},{8,0},{1,9},{9,1},{2,10},{10,2},{3,11},{11,3},{4,12},{12,4},... | collective-permute-start | bytes 1179656 | tf_op jit(solution)/shard_map/cond/branch_2_fun/ppermute | solution.py:154
  34.2 2.4 %collective-permute-start.22 = (bf16[128,1536]{1,0:T(8,128)(2,1)S(1)}, bf16[128,1536]{1,0:T(8,128)(2,1)S(1)}, u32[]{:S(2)}, u32[]{:S(2)}) collective-permute-start(bf16[128,1536]{1,0:T(8,128)(2,1)S(1)} %collective-permute-done.20.refs_3_), channel_id=1, source_target_pairs={{0,8},{8,0},{1,9},{9,1},{2,10},{10,2},{3,11},{11,3},{4,12},{12,4},... | collective-permute-start | bytes 1179656 | tf_op jit(solution)/shard_map/cond/branch_2_fun/ppermute | solution.py:154
  37.8 7.0 %collective-permute-start.23 = (bf16[128,256]{1,0:T(8,128)(2,1)S(1)}, bf16[128,256]{1,0:T(8,128)(2,1)S(1)}, u32[]{:S(2)}, u32[]{:S(2)}) collective-permute-start(bf16[128,256]{1,0:T(8,128)(2,1)S(1)} %get-tuple-element.20), channel_id=1, source_target_pairs={{8,1},{0,24},{9,0},{1,25},{10,3},{2,28},{11,2},{3,29},{12,5},{4,26... | collective-permute-start | bytes 196616 | tf_op jit(solution)/shard_map/cond/branch_2_fun/ppermute | solution.py:154
  38.8 6.4 %collective-permute-start.24 = (bf16[128,256]{1,0:T(8,128)(2,1)S(1)}, bf16[128,256]{1,0:T(8,128)(2,1)S(1)}, u32[]{:S(2)}, u32[]{:S(2)}) collective-permute-start(bf16[128,256]{1,0:T(8,128)(2,1)S(1)} %get-tuple-element.21), channel_id=1, source_target_pairs={{8,3},{0,30},{9,2},{1,31},{10,1},{2,26},{11,0},{3,27},{12,7},{4,28... | collective-permute-start | bytes 196616 | tf_op jit(solution)/shard_map/cond/branch_2_fun/ppermute | solution.py:154
  38.8 6.4 %collective-permute-start.25 = (bf16[128,256]{1,0:T(8,128)(2,1)S(1)}, bf16[128,256]{1,0:T(8,128)(2,1)S(1)}, u32[]{:S(2)}, u32[]{:S(2)}) collective-permute-start(bf16[128,256]{1,0:T(8,128)(2,1)S(1)} %get-tuple-element.22), channel_id=1, source_target_pairs={{0,0},{8,24},{1,1},{9,25},{2,2},{10,28},{3,3},{11,29},{4,4},{12,26... | collective-permute-start | bytes 196616 | tf_op jit(solution)/shard_map/cond/branch_2_fun/ppermute | solution.py:154
  41.9 6.0 %collective-permute-start.26 = (bf16[128,256]{1,0:T(8,128)(2,1)S(1)}, bf16[128,256]{1,0:T(8,128)(2,1)S(1)}, u32[]{:S(2)}, u32[]{:S(2)}) collective-permute-start(bf16[128,256]{1,0:T(8,128)(2,1)S(1)} %get-tuple-element.23), channel_id=1, source_target_pairs={{0,2},{8,30},{1,3},{9,31},{2,0},{10,26},{3,1},{11,27},{4,6},{12,28... | collective-permute-start | bytes 196616 | tf_op jit(solution)/shard_map/cond/branch_2_fun/ppermute | solution.py:154
  48.5 0.7 %copy-start.1 = (bf16[1,128,1024]{2,1,0:T(8,128)(2,1)}, bf16[1,128,1024]{2,1,0:T(8,128)(2,1)S(1)}, u32[]{:S(2)}) copy-start(bf16[1,128,1024]{2,1,0:T(8,128)(2,1)S(1)} %get-tuple-element.84) | copy-start | bytes 786436

commit v5 on v4

--- a/solution.py
+++ b/solution.py
@@ -33,45 +33,67 @@
 
 def flipped(half, place):
     low, high = half.bit_length() - 1, half.bit_length()
-    return ((place >> low) ^ (place >> high)) & 1
-
-
-def standard_kernel(people_all, *refs):
-    counts, rows_ref, out_ref = refs[:-2], refs[-2], refs[-1]
-    totals = counts[0][...]
-    for part in counts[1:]:
-        totals = totals + part[...]
-    freq = (totals.astype(jnp.float32) + 1.0) / (2.0 * people_all + 2.0)
-    scale = 1.0 / jnp.sqrt(2.0 * freq * (1.0 - freq))
-    rows = rows_ref[...].astype(jnp.float32)
-    out_ref[...] = ((rows - 2.0 * freq) * scale).astype(jnp.bfloat16)
-
-
-def standard_rows(rows, counts, people_all):
+    return 1 ^ ((place >> low) ^ (place >> high)) & 1
+
+
+def load_kernel(rows_ref, out_ref, sem):
+    copy = pltpu.make_async_copy(rows_ref, out_ref, sem)
+    copy.start()
+    copy.wait()
+
+
+def load_rows(rows):
+    return pl.pallas_call(
+        load_kernel,
+        out_shape=jax.ShapeDtypeStruct(rows.shape, rows.dtype),
+        in_specs=[pl.BlockSpec(memory_space=pltpu.HBM)],
+        out_specs=pl.BlockSpec(memory_space=pltpu.VMEM),
+        scratch_shapes=[pltpu.SemaphoreType.DMA],
+        compiler_params=pltpu.CompilerParams(vmem_limit_bytes=VMEM_BYTES),
+    )(rows)
+
+
+def sum_kernel(*refs):
+    total = refs[0][...]
+    for ref in refs[1:-1]:
+        total = total + ref[...]
+    refs[-1][...] = total
+
+
+def sum_of(parts):
     vmem = pl.BlockSpec(memory_space=pltpu.VMEM)
     return pl.pallas_call(
-        functools.partial(standard_kernel, people_all),
-        out_shape=jax.ShapeDtypeStruct(rows.shape, jnp.bfloat16),
-        in_specs=[vmem] * (len(counts) + 1),
+        sum_kernel,
+        out_shape=jax.ShapeDtypeStruct(parts[0].shape, parts[0].dtype),
+        in_specs=[vmem] * len(parts),
         out_specs=vmem,
         compiler_params=pltpu.CompilerParams(vmem_limit_bytes=VMEM_BYTES),
-    )(*counts, rows)
-
-
-def multiply_kernel(half, root, role_ref, *refs):
-    shards, send_ref, keep_ref = refs[: 3 * half], refs[3 * half : 4 * half], refs[4 * half :]
-    across = shards[:half]
-    fetched, passed = shards[half : 2 * half], shards[2 * half :]
-    rows = across[0].shape[0]
-
-    def product(first, second):
+    )(*parts)
+
+
+def multiply_kernel(half, people_all, role_ref, *refs):
+    groups = [refs[n * half : (n + 1) * half] for n in range(7)]
+    first, second, third, direct, crossed, send_ref, keep_ref = groups
+    rows, markers = first[0].shape
+    root = math.sqrt(markers)
+
+    def standard(parts, counts):
+        totals = counts[0][...]
+        for part in counts[1:]:
+            totals = totals + part[...]
+        freq = (totals.astype(jnp.float32) + 1.0) / (2.0 * people_all + 2.0)
+        scale = 1.0 / jnp.sqrt(2.0 * freq * (1.0 - freq))
+        whole = jnp.concatenate([part[...] for part in parts], axis=0)
+        return ((whole.astype(jnp.float32) - 2.0 * freq) * scale).astype(jnp.bfloat16)
+
+    def product(one, other):
         dims = (((1,), (1,)), ((), ()))
-        out = lax.dot_general(first, second, dims, preferred_element_type=jnp.float32)
+        out = lax.dot_general(one, other, dims, preferred_element_type=jnp.float32)
         return (out / root).astype(jnp.bfloat16)
 
-    def store(lefts, rights, left_ref, right_ref):
-        left_all = jnp.concatenate([part[...] for part in lefts], axis=0)
-        right_all = jnp.concatenate([part[...] for part in rights], axis=0)
+    def store(lefts, left_counts, rights, right_counts, left_ref, right_ref):
+        left_all = standard(lefts, left_counts)
+        right_all = standard(rights, right_counts)
         by_left = product(left_all, right_all)
         by_right = product(right_all, left_all)
         for t in range(half):
@@ -80,26 +102,26 @@
 
     @pl.when(role_ref[0] == 1)
     def _():
-        store(across, fetched, keep_ref, send_ref)
+        store(first, direct, second, crossed, keep_ref, send_ref)
 
     @pl.when(role_ref[0] == 0)
     def _():
-        store(fetched, passed, send_ref, keep_ref)
-
-
-def multiply(role, half, across, fetched, passed):
-    rows, markers = across[0].shape
-    shards = [*across, *fetched, *passed]
+        store(second, crossed, third[:1] + first[1:], direct, send_ref, keep_ref)
+
+
+def multiply(role, half, people_all, *groups):
+    shards = [array for group in groups for array in group]
+    rows = shards[0].shape[0]
     vmem = pl.BlockSpec(memory_space=pltpu.VMEM)
     block = jax.ShapeDtypeStruct((rows, half * rows), jnp.bfloat16)
     outs = pl.pallas_call(
-        functools.partial(multiply_kernel, half, math.sqrt(markers)),
+        functools.partial(multiply_kernel, half, people_all),
         out_shape=[block] * (2 * half),
         in_specs=[pl.BlockSpec(memory_space=pltpu.SMEM)] + [vmem] * len(shards),
         out_specs=[vmem] * (2 * half),
         compiler_params=pltpu.CompilerParams(vmem_limit_bytes=VMEM_BYTES),
     )(role, *shards)
-    return outs[:half], outs[half:]
+    return list(outs[:half]), list(outs[half:])
 
 
 def place_kernel(half, role_ref, *refs):
@@ -140,7 +162,7 @@
     )(role, *sent, *kept)
 
 
-def one_round(round_number, cohorts, blocks, own):
+def one_round(round_number, cohorts, blocks, own, beside, near_counts):
     half = half_size(blocks)
     left = left_cohorts(cohorts, round_number)
 
@@ -165,11 +187,20 @@
     def mate_to_left(d):
         return lambda c, i: ((c ^ 1, i), (c, i ^ d))
 
-    def mate_to_mate(c, i):
-        return (c ^ 1, i), (c ^ 1, i)
-
-    def owner_to_left(t):
-        return lambda c, i: ((c ^ round_number, right(i, t)), (c, i))
+    def mate_to_mate(d):
+        return lambda c, i: ((c ^ 1, i), (c ^ 1, i ^ d))
+
+    def owner_to_left(d):
+        return lambda c, i: ((c ^ round_number, i), (c, i ^ d))
+
+    def owner_to_mate(d):
+        return lambda c, i: ((c ^ round_number, i), (c ^ 1, i ^ d))
+
+    def right_rows_to_mate(t):
+        return lambda c, i: ((c ^ 1, i), (c ^ round_number, right(i, t)))
+
+    def right_rows_to_left(t):
+        return lambda c, i: ((c, i), (c ^ 1 ^ round_number, right(i, t)))
 
     def left_to_owner(t):
         return lambda c, i: ((c, i), (c ^ round_number, right(i, t)))
@@ -181,11 +212,20 @@
     is_left = functools.reduce(jnp.logical_or, [cohort == c for c in left])
     role = jnp.stack([is_left.astype(jnp.int32), lax.axis_index("person")])
 
-    across = [own] + [send(own, left_to_left(2 * t), mate_to_mate) for t in range(1, half)]
-    fetched = [send(across[t], left_to_mate(1), owner_to_left(t)) for t in range(half)]
-    passed = [send(fetched[t], left_to_mate(0), mate_to_left(0)) for t in range(half)]
-    sent, kept = multiply(role, half, across, fetched, passed)
-    sent, kept = list(sent), list(kept)
+    first = [own] + [
+        send(own, left_to_left(2 * t), right_rows_to_mate(t)) for t in range(1, half)
+    ]
+    second = [send(beside, right_rows_to_left(0), mate_to_mate(1))]
+    direct, crossed = [], []
+    for m in range(half):
+        d = far_step(half, m)
+        direct.append(send(near_counts, left_to_left(d), owner_to_mate(d)))
+        crossed.append(send(near_counts, left_to_mate(d), owner_to_left(d)))
+    third = [send(second[0], left_to_mate(0), mate_to_left(0))]
+    third += [send(first[t], left_to_mate(1), mate_to_left(0)) for t in range(1, half)]
+    second += third[1:]
+    people_all = own.shape[0] * blocks
+    sent, kept = multiply(role, half, people_all, first, second, third, direct, crossed)
     for t in reversed(range(half)):
         sent[t] = send(sent[t], mate_to_left(2 * t + 1), left_to_owner(t))
         kept[t] = send(kept[t], left_to_left(2 * t), mate_to_owner(t))
@@ -194,21 +234,18 @@
 
 def on_device(dosages, allele_counts, partner):
     cohorts, blocks = lax.axis_size("cohort"), lax.axis_size("person")
-    half = half_size(blocks)
-
-    def swap(value, step):
-        return lax.ppermute(value, "person", [(i, i ^ step) for i in range(blocks)])
-
-    near = allele_counts[0]
-    for step in range(1, 2 * half):
-        near = near + swap(allele_counts[0], step)
-    counts = [near] + [swap(near, far_step(half, m)) for m in range(1, half)]
-    own = standard_rows(dosages[0], counts, dosages.shape[1] * blocks)
+    counts = allele_counts[0]
+    near = [counts]
+    for step in range(1, 2 * half_size(blocks)):
+        near.append(lax.ppermute(counts, "person", [(i, i ^ step) for i in range(blocks)]))
+    own = load_rows(dosages[0])
+    beside = lax.ppermute(own, "cohort", [(c, c ^ 1) for c in range(cohorts)])
+    near_counts = sum_of(near)
     rounds = [
         functools.partial(one_round, round_number, cohorts, blocks)
         for round_number in range(1, cohorts)
     ]
-    return lax.switch(partner[0] - 1, rounds, own)
+    return lax.switch(partner[0] - 1, rounds, own, beside, near_counts)
 
 
 def solution(mesh):

time: 49.6 us -> 45.7 us (0.921)
  starting transfers between devices: 32.1 us -> 29.1 us
  other arithmetic: 0.78 us -> 0.08 us
    ppermute x4, starting transfers between devices: 7.05 us -> 3.8 us  [the longest x3 3.68 us: on_device(): lax.ppermute(counts, 'person', [(i, i ^ step) for i in range(blocks)])]
    ppermute x4, waiting for transfers between devices: 3.54 us -> 2.26 us  [the longest x3 2.25 us: on_device(): lax.ppermute(counts, 'person', [(i, i ^ step) for i in range(blocks)])]
    ppermute x9 -> x12, waiting for transfers between devices: 9.12 us -> 10 us  [send(): return lax.ppermute(value, AXES, pairs)]
    add x1 -> x0, other arithmetic: 0.7 us -> none  [on_device(): near = near + swap(allele_counts[0], step)]
    unnamed x6 -> x8, local copies, waits for them, and re-layouts: 1.7 us -> 2.06 us
    ppermute x9 -> x12, starting transfers between devices: 25 us -> 25.3 us  [send(): return lax.ppermute(value, AXES, pairs)]
    pallas_call x2 -> x3, Pallas kernels: 1.25 us -> 1.38 us  [the longest x1 1.18 us: multiply(): pl.pallas_call(functools.partial(multiply_kernel, half, people_all), out_...]
  transfers between devices with their start and end apart: 13 -> 16, of which waited for: 7 -> 9; matrix products, arithmetic and copies ran while one was open for 0% -> 0% of each run, Pallas kernels for 0% -> 0%
where the time goes in v5:
time: 45.7 us
  starting transfers between devices  29.1 us (64%)
  waiting for transfers between devices  12.3 us (27%)
  local copies, waits for them, and re-layouts  2.06 us (5%)
  Pallas kernels  2 us (4%)
    ppermute x12, starting transfers between devices, send(): return lax.ppermute(value, AXES, pairs)  25.3 us
    ppermute x12, waiting for transfers between devices, send(): return lax.ppermute(value, AXES, pairs)  10 us
    ppermute x3, starting transfers between devices, on_device(): lax.ppermute(counts, 'person', [(i, i ^ step) for i in range(blocks)])  3.68 us
    ppermute x3, waiting for transfers between devices, on_device(): lax.ppermute(counts, 'person', [(i, i ^ step) for i in range(blocks)])  2.25 us
    unnamed x8, local copies, waits for them, and re-layouts  2.06 us
    pallas_call x1, Pallas kernels, multiply(): pl.pallas_call(functools.partial(multiply_kernel, half, people_all), out_...  1.18 us
  transfers between devices with their start and end apart: 16, of which 9 were waited for; matrix products, arithmetic and copies ran while one was open for 0% of the time, Pallas kernels for 0%

profile of v5, /device:TPU:1, one launch (start us, length us, event | category | flops | bytes accessed | tf_op | source)
XLA Modules:
  0.0 45.7 jit_solution(11721125527745123248)
XLA Ops:
  0.0 0.0 copy-start
  0.0 1.0 %copy-done = bf16[1,128,1536]{2,1,0:T(8,128)(2,1)S(1)} copy-done((bf16[1,128,1536]{2,1,0:T(8,128)(2,1)S(1)}, bf16[1,128,1536]{2,1,0:T(8,128)(2,1)}, u32[]{:S(2)}) %copy-start) | copy-done | bytes 393240
  1.0 0.0 copy-start.1
  1.0 0.2 shard_map.40
  1.2 0.1 collective-permute-start.36
  1.3 0.4 copy-done.1
  1.7 0.0 copy-start.3
  1.7 3.3 %collective-permute-start.39 = (s32[1,1536]{1,0:T(1,128)S(1)}, s32[1,1536]{1,0:T(1,128)S(1)}, u32[]{:S(2)}, u32[]{:S(2)}) collective-permute-start(s32[1,1536]{1,0:T(1,128)S(1)} %bitcast.11), channel_id=1, source_target_pairs={{0,3},{1,2},{2,1},{3,0},{4,7},{5,6},{6,5},{7,4},{8,11},{9,10},{10,... | collective-permute-start | bytes 18440 | tf_op jit(solution)/shard_map/ppermute | solution.py:240
  5.0 0.2 collective-permute-start.38
  5.2 0.2 collective-permute-start.37
  5.4 0.0 copy-done.3
  5.4 0.6 %collective-permute-done.39.refs_3_ = s32[1,1536]{1,0:T(1,128)S(1)} collective-permute-done((s32[1,1536]{1,0:T(1,128)S(1)}, s32[1,1536]{1,0:T(1,128)S(1)}, u32[]{:S(2)}, u32[]{:S(2)}) %collective-permute-start.39) | collective-permute-done | bytes 6176 | tf_op jit(solution)/shard_map/ppermute | solution.py:240
  6.0 1.5 %collective-permute-done.38.refs_2_ = s32[1,1536]{1,0:T(1,128)S(1)} collective-permute-done((s32[1,1536]{1,0:T(1,128)S(1)}, s32[1,1536]{1,0:T(1,128)S(1)}, u32[]{:S(2)}, u32[]{:S(2)}) %collective-permute-start.38) | collective-permute-done | bytes 6176 | tf_op jit(solution)/shard_map/ppermute | solution.py:240
  7.5 0.2 collective-permute-done.37.refs_1_
  7.7 0.0 collective-permute-done.36
  7.7 37.3 %conditional.1 = (bf16[1,128,1024]{2,1,0:T(8,128)(2,1)S(1)}) conditional(s32[]{:T(128)} %bitcast.6, (bf16[128,1536]{1,0:T(8,128)(2,1)S(1)}, bf16[128,1536]{1,0:T(8,128)(2,1)S(1)}, s32[1,1536]{1,0:T(1,128)S(1)}) %tuple.14, (bf16[128,1536]{1,0:T(8,128)(2,1)S(1)}, bf16[128,1536]{1,0:T(8,128)(2,1)S(1)}, ...), branch_computations={%region_0.0_spmd, %region_1.0_spmd, %region_2.0_spmd} | conditional | flops 11 | bytes 7438918 | solution.py:248
  7.7 0.5 %collective-permute-start.13 = (bf16[128,1536]{1,0:T(8,128)(2,1)S(1)}, bf16[128,1536]{1,0:T(8,128)(2,1)S(1)}, u32[]{:S(2)}, u32[]{:S(2)}) collective-permute-start(bf16[128,1536]{1,0:T(8,128)(2,1)S(1)} %get-tuple-element.35), channel_id=1, source_target_pairs={{0,30},{8,9},{1,31},{9,8},{2,26},{10,11},{3,27},{11,10},{4,28},{12... | collective-permute-start | bytes 1179656 | tf_op jit(solution)/shard_map/cond/branch_1_fun/ppermute | solution.py:176
  8.3 3.3 %collective-permute-start.12 = (bf16[128,1536]{1,0:T(8,128)(2,1)S(1)}, bf16[128,1536]{1,0:T(8,128)(2,1)S(1)}, u32[]{:S(2)}, u32[]{:S(2)}) collective-permute-start(bf16[128,1536]{1,0:T(8,128)(2,1)S(1)} %get-tuple-element.34.refs_0_), channel_id=1, source_target_pairs={{0,2},{8,16},{1,3},{9,17},{2,0},{10,20},{3,1},{11,21},{4,6},{12,18... | collective-permute-start | bytes 1179656 | tf_op jit(solution)/shard_map/cond/branch_1_fun/ppermute | solution.py:176
  11.5 2.9 %collective-permute-done.13.refs_2_ = bf16[128,1536]{1,0:T(8,128)(2,1)S(1)} collective-permute-done((bf16[128,1536]{1,0:T(8,128)(2,1)S(1)}, bf16[128,1536]{1,0:T(8,128)(2,1)S(1)}, u32[]{:S(2)}, u32[]{:S(2)}) %collective-permute-start.13) | collective-permute-done | bytes 393248 | tf_op jit(solution)/shard_map/cond/branch_1_fun/ppermute | solution.py:176
  14.4 5.7 %collective-permute-start.15 = (bf16[128,1536]{1,0:T(8,128)(2,1)S(1)}, bf16[128,1536]{1,0:T(8,128)(2,1)S(1)}, u32[]{:S(2)}, u32[]{:S(2)}) collective-permute-start(bf16[128,1536]{1,0:T(8,128)(2,1)S(1)} %collective-permute-done.13.refs_2_), channel_id=1, source_target_pairs={{0,8},{8,0},{1,9},{9,1},{2,10},{10,2},{3,11},{11,3},{4,12},{12,4},... | collective-permute-start | bytes 1179656 | tf_op jit(solution)/shard_map/cond/branch_1_fun/ppermute | solution.py:176
  20.1 1.4 %collective-permute-done.12.refs_1_ = bf16[128,1536]{1,0:T(8,128)(2,1)S(1)} collective-permute-done((bf16[128,1536]{1,0:T(8,128)(2,1)S(1)}, bf16[128,1536]{1,0:T(8,128)(2,1)S(1)}, u32[]{:S(2)}, u32[]{:S(2)}) %collective-permute-start.12) | collective-permute-done | bytes 393248 | tf_op jit(solution)/shard_map/cond/branch_1_fun/ppermute | solution.py:176
  21.5 2.1 %collective-permute-start.14 = (bf16[128,1536]{1,0:T(8,128)(2,1)S(1)}, bf16[128,1536]{1,0:T(8,128)(2,1)S(1)}, u32[]{:S(2)}, u32[]{:S(2)}) collective-permute-start(bf16[128,1536]{1,0:T(8,128)(2,1)S(1)} %collective-permute-done.12.refs_1_), channel_id=1, source_target_pairs={{0,9},{8,0},{1,8},{9,1},{2,11},{10,2},{3,10},{11,3},{4,13},{12,4},... | collective-permute-start | bytes 1179656 | tf_op jit(solution)/shard_map/cond/branch_1_fun/ppermute | solution.py:176
  23.6 3.6 %collective-permute-start.19 = (s32[1,1536]{1,0:T(1,128)S(1)}, s32[1,1536]{1,0:T(1,128)S(1)}, u32[]{:S(2)}, u32[]{:S(2)}) collective-permute-start(s32[1,1536]{1,0:T(1,128)S(1)} %get-tuple-element.36), channel_id=1, source_target_pairs={{0,14},{16,6},{1,15},{17,7},{2,12},{18,4},{3,13},{19,5},{4,10},{20... | collective-permute-start | bytes 18440 | tf_op jit(solution)/shard_map/cond/branch_1_fun/ppermute | solution.py:176
  27.2 0.0 collective-permute-start.18
  27.2 1.4 %collective-permute-start.17 = (s32[1,1536]{1,0:T(1,128)S(1)}, s32[1,1536]{1,0:T(1,128)S(1)}, u32[]{:S(2)}, u32[]{:S(2)}) collective-permute-start(s32[1,1536]{1,0:T(1,128)S(1)} %get-tuple-element.36), channel_id=1, source_target_pairs={{0,6},{16,14},{1,7},{17,15},{2,4},{18,12},{3,5},{19,13},{4,2},{20,... | collective-permute-start | bytes 18440 | tf_op jit(solution)/shard_map/cond/branch_1_fun/ppermute | solution.py:176
  28.6 0.0 collective-permute-done.19.refs_9_
  28.6 2.4 %collective-permute-start.16 = (s32[1,1536]{1,0:T(1,128)S(1)}, s32[1,1536]{1,0:T(1,128)S(1)}, u32[]{:S(2)}, u32[]{:S(2)}) collective-permute-start(s32[1,1536]{1,0:T(1,128)S(1)} %get-tuple-element.36), channel_id=1, source_target_pairs={{0,0},{16,8},{1,1},{17,9},{2,2},{18,10},{3,3},{19,11},{4,4},{20,12... | collective-permute-start | bytes 18440 | tf_op jit(solution)/shard_map/cond/branch_1_fun/ppermute | solution.py:176
  31.0 0.1 pad_add_fusion.1.role_ref
  31.1 0.0 collective-permute-done.18.refs_8_
  31.1 1.9 %collective-permute-done.17.refs_7_ = s32[1,1536]{1,0:T(1,128)S(1)} collective-permute-done((s32[1,1536]{1,0:T(1,128)S(1)}, s32[1,1536]{1,0:T(1,128)S(1)}, u32[]{:S(2)}, u32[]{:S(2)}) %collective-permute-start.17) | collective-permute-done | bytes 6176 | tf_op jit(solution)/shard_map/cond/branch_1_fun/ppermute | solution.py:176
  33.0 0.5 %collective-permute-done.16.refs_6_ = s32[1,1536]{1,0:T(1,128)S(1)} collective-permute-done((s32[1,1536]{1,0:T(1,128)S(1)}, s32[1,1536]{1,0:T(1,128)S(1)}, u32[]{:S(2)}, u32[]{:S(2)}) %collective-permute-start.16) | collective-permute-done | bytes 6176 | tf_op jit(solution)/shard_map/cond/branch_1_fun/ppermute | solution.py:176
  33.5 0.0 collective-permute-done.15.refs_4_
  33.5 0.0 collective-permute-done.14.refs_3_.refs_5_
  33.5 1.2 %branch_1_fun.2 = (bf16[128,256]{1,0:T(8,128)(2,1)S(1)}, bf16[128,256]{1,0:T(8,128)(2,1)S(1)}, bf16[128,256]{1,0:T(8,128)(2,1)S(1)}, bf16[128,256]{1,0:T(8,128)(2,1)S(1)}) custom-call(s32[2]{0:T(128)S(1)} %pad_add_fusion.1.role_ref, bf16[128,1536]{1,0:T(8,128)(2,1)S(1)} %get-tuple-element.34.refs_0_, bf16[128,1536]{1,0:T(8,128)(2,1)S(1)} %collective-permute-done.12.refs_1_, ...), custom_call_target="tpu_custom_call" | custom-call | tf_op jit(solution)/shard_map/cond/branch_1_fun/pallas_call | solution.py:117
  34.7 0.1 collective-permute-start.20
  34.8 0.9 %collective-permute-start.21 = (bf16[128,256]{1,0:T(8,128)(2,1)S(1)}, bf16[128,256]{1,0:T(8,128)(2,1)S(1)}, u32[]{:S(2)}, u32[]{:S(2)}) collective-permute-start(bf16[128,256]{1,0:T(8,128)(2,1)S(1)} %get-tuple-element.38), channel_id=1, source_target_pairs={{8,3},{0,16},{9,2},{1,17},{10,1},{2,20},{11,0},{3,21},{12,7},{4,18... | collective-permute-start | bytes 196616 | tf_op jit(solution)/shard_map/cond/branch_1_fun/ppermute | solution.py:176
  35.7 4.2 %collective-permute-start.22 = (bf16[128,256]{1,0:T(8,128)(2,1)S(1)}, bf16[128,256]{1,0:T(8,128)(2,1)S(1)}, u32[]{:S(2)}, u32[]{:S(2)}) collective-permute-start(bf16[128,256]{1,0:T(8,128)(2,1)S(1)} %get-tuple-element.39), channel_id=1, source_target_pairs={{0,0},{8,22},{1,1},{9,23},{2,2},{10,18},{3,3},{11,19},{4,4},{12,20... | collective-permute-start | bytes 196616 | tf_op jit(solution)/shard_map/cond/branch_1_fun/ppermute | solution.py:176
  39.9 1.2 %collective-permute-start.23 = (bf16[128,256]{1,0:T(8,128)(2,1)S(1)}, bf16[128,256]{1,0:T(8,128)(2,1)S(1)}, u32[]{:S(2)}, u32[]{:S(2)}) collective-permute-start(bf16[128,256]{1,0:T(8,128)(2,1)S(1)} %get-tuple-element.40), channel_id=1, source_target_pairs={{0,2},{8,16},{1,3},{9,17},{2,0},{10,20},{3,1},{11,21},{4,6},{12,18... | collective-permute-start | bytes 196616 | tf_op jit(solution)/shard_map/cond/branch_1_fun/ppermute | solution.py:176
  41.1 0.0 collective-permute-done.20.refs_0_
  41.1 0.0 collective-permute-done.21.refs_1_
  41.1 3.0 %collective-permute-done.22.refs_2_ = bf16[128,256]{1,0:T(8,128)(2,1)S(1)} collective-permute-done((bf16[128,256]{1,0:T(8,128)(2,1)S(1)}, bf16[128,256]{1,0:T(8,128)(2,1)S(1)}, u32[]{:S(2)}, u32[]{:S(2)}) %collective-permute-start.22) | collective-permute-done | bytes 65568 | tf_op jit(solution)/shard_map/cond/branch_1_fun/ppermute | solution.py:176
  44.1 0.3 collective-permute-done.23.refs_3_
  44.3 0.6 %branch_1_fun.3 = bf16[1,128,1024]{2,1,0:T(8,128)(2,1)S(1)} custom-call(s32[2]{0:T(128)S(1)} %pad_add_fusion.1.role_ref, bf16[128,256]{1,0:T(8,128)(2,1)S(1)} %collective-permute-done.20.refs_0_, bf16[128,256]{1,0:T(8,128)(2,1)S(1)} %collective-permute-done.21.refs_1_, bf16[128,256]{1,0:T(8,128)(2,1)S(1)} %collective-permute-done.22.refs_2_, ...), custom_call_target="tpu_custom_call" | custom-call | tf_op jit(solution)/shard_map/cond/branch_1_fun/pallas_call | solution.py:156
  45.0 0.0 copy-start.2
  45.0 0.7 %copy-done.2 = bf16[1,128,1024]{2,1,0:T(8,128)(2,1)} copy-done((bf16[1,128,1024]{2,1,0:T(8,128)(2,1)}, bf16[1,128,1024]{2,1,0:T(8,128)(2,1)S(1)}, u32[]{:S(2)}) %copy-start.2) | copy-done | bytes 262168
  (1 shorter events, 0.0 us)
Async XLA Ops:
  0.0 1.0 %copy-start = (bf16[1,128,1536]{2,1,0:T(8,128)(2,1)S(1)}, bf16[1,128,1536]{2,1,0:T(8,128)(2,1)}, u32[]{:S(2)}) copy-start(bf16[1,128,1536]{2,1,0:T(8,128)(2,1)} %param.6) | copy-start | bytes 1179652
  1.0 0.7 %copy-start.1 = (s32[1,1,1536]{2,1,0:T(1,128)S(1)}, s32[1,1,1536]{2,1,0:T(1,128)}, u32[]{:S(2)}) copy-start(s32[1,1,1536]{2,1,0:T(1,128)} %param.7) | copy-start | bytes 18436
  1.2 6.5 %collective-permute-start.36 = (bf16[128,1536]{1,0:T(8,128)(2,1)S(1)}, bf16[128,1536]{1,0:T(8,128)(2,1)S(1)}, u32[]{:S(2)}, u32[]{:S(2)}) collective-permute-start(bf16[128,1536]{1,0:T(8,128)(2,1)S(1)} %shard_map.40), channel_id=1, source_target_pairs={{0,8},{8,0},{16,24},{24,16},{1,9},{9,1},{17,25},{25,17},{2,10},{10... | collective-permute-start | bytes 1179656 | tf_op jit(solution)/shard_map/ppermute | solution.py:242
  1.7 3.7 %copy-start.3 = (s32[4]{0:T(128)S(1)}, s32[4]{0:T(128)}, u32[]{:S(2)}) copy-start(s32[4]{0:T(128)} %param.8) | copy-start | bytes 52
  1.7 4.4 %collective-permute-start.39 = (s32[1,1536]{1,0:T(1,128)S(1)}, s32[1,1536]{1,0:T(1,128)S(1)}, u32[]{:S(2)}, u32[]{:S(2)}) collective-permute-start(s32[1,1536]{1,0:T(1,128)S(1)} %bitcast.11), channel_id=1, source_target_pairs={{0,3},{1,2},{2,1},{3,0},{4,7},{5,6},{6,5},{7,4},{8,11},{9,10},{10,... | collective-permute-start | bytes 18440 | tf_op jit(solution)/shard_map/ppermute | solution.py:240
  5.0 2.5 %collective-permute-start.38 = (s32[1,1536]{1,0:T(1,128)S(1)}, s32[1,1536]{1,0:T(1,128)S(1)}, u32[]{:S(2)}, u32[]{:S(2)}) collective-permute-start(s32[1,1536]{1,0:T(1,128)S(1)} %bitcast.12), channel_id=1, source_target_pairs={{0,2},{1,3},{2,0},{3,1},{4,6},{5,7},{6,4},{7,5},{8,10},{9,11},{10,... | collective-permute-start | bytes 18440 | tf_op jit(solution)/shard_map/ppermute | solution.py:240
  5.2 2.5 %collective-permute-start.37 = (s32[1,1536]{1,0:T(1,128)S(1)}, s32[1,1536]{1,0:T(1,128)S(1)}, u32[]{:S(2)}, u32[]{:S(2)}) collective-permute-start(s32[1,1536]{1,0:T(1,128)S(1)} %bitcast.13), channel_id=1, source_target_pairs={{0,1},{1,0},{2,3},{3,2},{4,5},{5,4},{6,7},{7,6},{8,9},{9,8},{10,11... | collective-permute-start | bytes 18440 | tf_op jit(solution)/shard_map/ppermute | solution.py:240
  7.7 6.7 %collective-permute-start.13 = (bf16[128,1536]{1,0:T(8,128)(2,1)S(1)}, bf16[128,1536]{1,0:T(8,128)(2,1)S(1)}, u32[]{:S(2)}, u32[]{:S(2)}) collective-permute-start(bf16[128,1536]{1,0:T(8,128)(2,1)S(1)} %get-tuple-element.35), channel_id=1, source_target_pairs={{0,30},{8,9},{1,31},{9,8},{2,26},{10,11},{3,27},{11,10},{4,28},{12... | collective-permute-start | bytes 1179656 | tf_op jit(solution)/shard_map/cond/branch_1_fun/ppermute | solution.py:176
  8.3 13.2 %collective-permute-start.12 = (bf16[128,1536]{1,0:T(8,128)(2,1)S(1)}, bf16[128,1536]{1,0:T(8,128)(2,1)S(1)}, u32[]{:S(2)}, u32[]{:S(2)}) collective-permute-start(bf16[128,1536]{1,0:T(8,128)(2,1)S(1)} %get-tuple-element.34.refs_0_), channel_id=1, source_target_pairs={{0,2},{8,16},{1,3},{9,17},{2,0},{10,20},{3,1},{11,21},{4,6},{12,18... | collective-permute-start | bytes 1179656 | tf_op jit(solution)/shard_map/cond/branch_1_fun/ppermute | solution.py:176
  14.4 19.1 %collective-permute-start.15 = (bf16[128,1536]{1,0:T(8,128)(2,1)S(1)}, bf16[128,1536]{1,0:T(8,128)(2,1)S(1)}, u32[]{:S(2)}, u32[]{:S(2)}) collective-permute-start(bf16[128,1536]{1,0:T(8,128)(2,1)S(1)} %collective-permute-done.13.refs_2_), channel_id=1, source_target_pairs={{0,8},{8,0},{1,9},{9,1},{2,10},{10,2},{3,11},{11,3},{4,12},{12,4},... | collective-permute-start | bytes 1179656 | tf_op jit(solution)/shard_map/cond/branch_1_fun/ppermute | solution.py:176
  21.5 12.0 %collective-permute-start.14 = (bf16[128,1536]{1,0:T(8,128)(2,1)S(1)}, bf16[128,1536]{1,0:T(8,128)(2,1)S(1)}, u32[]{:S(2)}, u32[]{:S(2)}) collective-permute-start(bf16[128,1536]{1,0:T(8,128)(2,1)S(1)} %collective-permute-done.12.refs_1_), channel_id=1, source_target_pairs={{0,9},{8,0},{1,8},{9,1},{2,11},{10,2},{3,10},{11,3},{4,13},{12,4},... | collective-permute-start | bytes 1179656 | tf_op jit(solution)/shard_map/cond/branch_1_fun/ppermute | solution.py:176
  23.6 5.0 %collective-permute-start.19 = (s32[1,1536]{1,0:T(1,128)S(1)}, s32[1,1536]{1,0:T(1,128)S(1)}, u32[]{:S(2)}, u32[]{:S(2)}) collective-permute-start(s32[1,1536]{1,0:T(1,128)S(1)} %get-tuple-element.36), channel_id=1, source_target_pairs={{0,14},{16,6},{1,15},{17,7},{2,12},{18,4},{3,13},{19,5},{4,10},{20... | collective-permute-start | bytes 18440 | tf_op jit(solution)/shard_map/cond/branch_1_fun/ppermute | solution.py:176
  27.2 3.9 %collective-permute-start.18 = (s32[1,1536]{1,0:T(1,128)S(1)}, s32[1,1536]{1,0:T(1,128)S(1)}, u32[]{:S(2)}, u32[]{:S(2)}) collective-permute-start(s32[1,1536]{1,0:T(1,128)S(1)} %get-tuple-element.36), channel_id=1, source_target_pairs={{0,8},{16,0},{1,9},{17,1},{2,10},{18,2},{3,11},{19,3},{4,12},{20,4... | collective-permute-start | bytes 18440 | tf_op jit(solution)/shard_map/cond/branch_1_fun/ppermute | solution.py:176
  27.2 5.8 %collective-permute-start.17 = (s32[1,1536]{1,0:T(1,128)S(1)}, s32[1,1536]{1,0:T(1,128)S(1)}, u32[]{:S(2)}, u32[]{:S(2)}) collective-permute-start(s32[1,1536]{1,0:T(1,128)S(1)} %get-tuple-element.36), channel_id=1, source_target_pairs={{0,6},{16,14},{1,7},{17,15},{2,4},{18,12},{3,5},{19,13},{4,2},{20,... | collective-permute-start | bytes 18440 | tf_op jit(solution)/shard_map/cond/branch_1_fun/ppermute | solution.py:176
  28.6 4.9 %collective-permute-start.16 = (s32[1,1536]{1,0:T(1,128)S(1)}, s32[1,1536]{1,0:T(1,128)S(1)}, u32[]{:S(2)}, u32[]{:S(2)}) collective-permute-start(s32[1,1536]{1,0:T(1,128)S(1)} %get-tuple-element.36), channel_id=1, source_target_pairs={{0,0},{16,8},{1,1},{17,9},{2,2},{18,10},{3,3},{19,11},{4,4},{20,12... | collective-permute-start | bytes 18440 | tf_op jit(solution)/shard_map/cond/branch_1_fun/ppermute | solution.py:176
  34.7 6.4 %collective-permute-start.20 = (bf16[128,256]{1,0:T(8,128)(2,1)S(1)}, bf16[128,256]{1,0:T(8,128)(2,1)S(1)}, u32[]{:S(2)}, u32[]{:S(2)}) collective-permute-start(bf16[128,256]{1,0:T(8,128)(2,1)S(1)} %get-tuple-element.37), channel_id=1, source_target_pairs={{8,1},{0,22},{9,0},{1,23},{10,3},{2,18},{11,2},{3,19},{12,5},{4,20... | collective-permute-start | bytes 196616 | tf_op jit(solution)/shard_map/cond/branch_1_fun/ppermute | solution.py:176
  34.8 6.3 %collective-permute-start.21 = (bf16[128,256]{1,0:T(8,128)(2,1)S(1)}, bf16[128,256]{1,0:T(8,128)(2,1)S(1)}, u32[]{:S(2)}, u32[]{:S(2)}) collective-permute-start(bf16[128,256]{1,0:T(8,128)(2,1)S(1)} %get-tuple-element.38), channel_id=1, source_target_pairs={{8,3},{0,16},{9,2},{1,17},{10,1},{2,20},{11,0},{3,21},{12,7},{4,18... | collective-permute-start | bytes 196616 | tf_op jit(solution)/shard_map/cond/branch_1_fun/ppermute | solution.py:176
  35.7 8.4 %collective-permute-start.22 = (bf16[128,256]{1,0:T(8,128)(2,1)S(1)}, bf16[128,256]{1,0:T(8,128)(2,1)S(1)}, u32[]{:S(2)}, u32[]{:S(2)}) collective-permute-start(bf16[128,256]{1,0:T(8,128)(2,1)S(1)} %get-tuple-element.39), channel_id=1, source_target_pairs={{0,0},{8,22},{1,1},{9,23},{2,2},{10,18},{3,3},{11,19},{4,4},{12,20... | collective-permute-start | bytes 196616 | tf_op jit(solution)/shard_map/cond/branch_1_fun/ppermute | solution.py:176
  39.9 4.5 %collective-permute-start.23 = (bf16[128,256]{1,0:T(8,128)(2,1)S(1)}, bf16[128,256]{1,0:T(8,128)(2,1)S(1)}, u32[]{:S(2)}, u32[]{:S(2)}) collective-permute-start(bf16[128,256]{1,0:T(8,128)(2,1)S(1)} %get-tuple-element.40), channel_id=1, source_target_pairs={{0,2},{8,16},{1,3},{9,17},{2,0},{10,20},{3,1},{11,21},{4,6},{12,18... | collective-permute-start | bytes 196616 | tf_op jit(solution)/shard_map/cond/branch_1_fun/ppermute | solution.py:176
  45.0 0.7 %copy-start.2 = (bf16[1,128,1024]{2,1,0:T(8,128)(2,1)}, bf16[1,128,1024]{2,1,0:T(8,128)(2,1)S(1)}, u32[]{:S(2)}) copy-start(bf16[1,128,1024]{2,1,0:T(8,128)(2,1)S(1)} %get-tuple-element.116) | copy-start | bytes 786436

commit v6 on v5

v6 whole, which is shorter than its diff:
```python
import functools
import math

import jax
import jax.numpy as jnp
from jax import lax
from jax.experimental import pallas as pl
from jax.experimental.pallas import tpu as pltpu
from jax.sharding import PartitionSpec as P

AXES = ("cohort", "person")
VMEM_BYTES = 48 * 1024 * 1024


def left_cohorts(cohorts, round_number):
    if round_number == 1:
        return [c for c in range(cohorts) if c & 1 == 0]
    top = 1 << (round_number.bit_length() - 1)
    return [
        c
        for c in range(cohorts)
        if (c & top == 0 and c & 1 == 0) or (c & top and (c ^ round_number ^ 1) & 1 == 0)
    ]


def half_size(blocks):
    return 1 << (blocks.bit_length() // 2 - 1)


def load_kernel(rows_ref, out_ref, sem):
    copy = pltpu.make_async_copy(rows_ref, out_ref, sem)
    copy.start()
    copy.wait()


def load_rows(rows):
    return pl.pallas_call(
        load_kernel,
        out_shape=jax.ShapeDtypeStruct(rows.shape, rows.dtype),
        in_specs=[pl.BlockSpec(memory_space=pltpu.HBM)],
        out_specs=pl.BlockSpec(memory_space=pltpu.VMEM),
        scratch_shapes=[pltpu.SemaphoreType.DMA],
        compiler_params=pltpu.CompilerParams(vmem_limit_bytes=VMEM_BYTES),
    )(rows)


def sum_kernel(parts_ref, out_ref):
    total = parts_ref[0]
    for n in range(1, parts_ref.shape[0]):
        total = total + parts_ref[n]
    out_ref[...] = total


def sum_of(parts):
    vmem = pl.BlockSpec(memory_space=pltpu.VMEM)
    return pl.pallas_call(
        sum_kernel,
        out_shape=jax.ShapeDtypeStruct(parts.shape[1:], parts.dtype),
        in_specs=[vmem],
        out_specs=vmem,
        compiler_params=pltpu.CompilerParams(vmem_limit_bytes=VMEM_BYTES),
    )(parts)


def multiply_kernel(half, people_all, role_ref, *refs):
    groups = [refs[n * half : (n + 1) * half] for n in range(3)]
    first, second, third = groups
    direct, crossed = refs[3 * half : 3 * half + 2]
    send_ref, keep_ref = refs[3 * half + 2 : 4 * half + 2], refs[4 * half + 2 :]
    rows, markers = first[0].shape
    root = math.sqrt(markers)

    def standard(parts, totals):
        freq = (totals[...].astype(jnp.float32) + 1.0) / (2.0 * people_all + 2.0)
        scale = 1.0 / jnp.sqrt(2.0 * freq * (1.0 - freq))
        whole = jnp.concatenate([part[...] for part in parts], axis=0)
        return ((whole.astype(jnp.float32) - 2.0 * freq) * scale).astype(jnp.bfloat16)

    def product(one, other):
        dims = (((1,), (1,)), ((), ()))
        out = lax.dot_general(one, other, dims, preferred_element_type=jnp.float32)
        return (out / root).astype(jnp.bfloat16)

    def store(lefts, left_totals, rights, right_totals, left_ref, right_ref):
        left_all = standard(lefts, left_totals)
        right_all = standard(rights, right_totals)
        by_left = product(left_all, right_all)
        by_right = product(right_all, left_all)
        for t in range(half):
            left_ref[t][...] = by_left[t * rows : (t + 1) * rows]
            right_ref[t][...] = by_right[t * rows : (t + 1) * rows]

    @pl.when(role_ref[0] == 1)
    def _():
        store(first, direct, second, crossed, keep_ref, send_ref)

    @pl.when(role_ref[0] == 0)
    def _():
        store(second, crossed, third[:1] + first[1:], direct, send_ref, keep_ref)


def multiply(role, people_all, first, second, third, direct, crossed):
    half = len(first)
    shards = [*first, *second, *third, direct, crossed]
    rows = shards[0].shape[0]
    vmem = pl.BlockSpec(memory_space=pltpu.VMEM)
    block = jax.ShapeDtypeStruct((rows, half * rows), jnp.bfloat16)
    outs = pl.pallas_call(
        functools.partial(multiply_kernel, half, people_all),
        out_shape=[block] * (2 * half),
        in_specs=[pl.BlockSpec(memory_space=pltpu.SMEM)] + [vmem] * len(shards),
        out_specs=[vmem] * (2 * half),
        compiler_params=pltpu.CompilerParams(vmem_limit_bytes=VMEM_BYTES),
    )(role, *shards)
    return list(outs[:half]), list(outs[half:])


def place_kernel(half, role_ref, *refs):
    sent, kept, out_ref = refs[:half], refs[half:-1], refs[-1]
    rows = out_ref.shape[1]
    place = role_ref[1]
    near = 2 * half

    def put(block, value):
        out_ref[0, :, pl.ds(pl.multiple_of(block * rows, rows), rows)] = value

    @pl.when(role_ref[0] == 1)
    def _():
        for t in range(half):
            for part, chip in ((kept[t], place ^ 2 * t), (sent[t], place ^ 2 * t + 1)):
                for m in range(half):
                    put(chip ^ near * m, part[:, m * rows : (m + 1) * rows])

    @pl.when(role_ref[0] == 0)
    def _():
        for t in range(half):
            chip = place ^ near * t
            for d in range(half):
                put(chip ^ 2 * d, sent[t][:, d * rows : (d + 1) * rows])
                put(chip ^ 2 * d + 1, kept[t][:, d * rows : (d + 1) * rows])


def place_blocks(role, half, sent, kept):
    rows = sent[0].shape[0]
    vmem = pl.BlockSpec(memory_space=pltpu.VMEM)
    return pl.pallas_call(
        functools.partial(place_kernel, half),
        out_shape=jax.ShapeDtypeStruct((1, rows, 2 * half * half * rows), jnp.bfloat16),
        in_specs=[pl.BlockSpec(memory_space=pltpu.SMEM)] + [vmem] * (2 * half),
        out_specs=vmem,
        compiler_params=pltpu.CompilerParams(vmem_limit_bytes=VMEM_BYTES),
    )(role, *sent, *kept)


def one_round(round_number, cohorts, blocks, own, counts):
    half = half_size(blocks)
    near = 2 * half
    left = left_cohorts(cohorts, round_number)

    def send(value, *legs):
        pairs = []
        for c in left:
            for i in range(blocks):
                for leg in legs:
                    (c0, i0), (c1, i1) = leg(c, i)
                    pairs.append((c0 * blocks + i0, c1 * blocks + i1))
        return lax.ppermute(value, AXES, pairs)

    def left_to_left(d):
        return lambda c, i: ((c, i), (c, i ^ d))

    def left_to_mate(d):
        return lambda c, i: ((c, i), (c ^ 1, i ^ d))

    def mate_to_left(d):
        return lambda c, i: ((c ^ 1, i), (c, i ^ d))

    def mate_to_mate(d):
        return lambda c, i: ((c ^ 1, i), (c ^ 1, i ^ d))

    def owner_to_left(c, i):
        return (c ^ round_number, i), (c, i)

    def owner_to_mate(c, i):
        return (c ^ round_number, i), (c ^ 1, i)

    def right_rows_to_mate(t):
        return lambda c, i: ((c ^ 1, i), (c ^ round_number, i ^ near * t))

    def right_rows_to_left(c, i):
        return (c, i), (c ^ 1 ^ round_number, i)

    def left_to_owner(t):
        return lambda c, i: ((c, i), (c ^ round_number, i ^ near * t))

    def mate_to_owner(t):
        return lambda c, i: ((c ^ 1, i), (c ^ round_number, i ^ near * t))

    cohort = lax.axis_index("cohort")
    is_left = functools.reduce(jnp.logical_or, [cohort == c for c in left])
    role = jnp.stack([is_left.astype(jnp.int32), lax.axis_index("person")])

    first = [own] + [
        send(own, left_to_left(2 * t), right_rows_to_mate(t)) for t in range(1, half)
    ]
    beside = send(own, left_to_mate(0), mate_to_left(0))
    second = [send(beside, right_rows_to_left, mate_to_mate(1))]
    counts, _ = lax.optimization_barrier((counts, beside))
    spread = jnp.broadcast_to(counts[None], (blocks, *counts.shape))
    totals = sum_of(lax.all_to_all(spread, "person", 0, 0, tiled=True))
    *first[1:], totals = lax.optimization_barrier((*first[1:], totals))
    crossed = send(totals, left_to_mate(0), owner_to_left)
    direct = totals
    if round_number != 1:
        direct = send(totals, left_to_left(0), owner_to_mate)
    third = [send(second[0], left_to_mate(0), mate_to_left(0))]
    third += [send(first[t], left_to_mate(1), mate_to_left(0)) for t in range(1, half)]
    second += third[1:]
    people_all = own.shape[0] * blocks
    sent, kept = multiply(role, people_all, first, second, third, direct, crossed)
    for t in reversed(range(half)):
        sent[t] = send(sent[t], mate_to_left(2 * t + 1), left_to_owner(t))
        if t or round_number != 1:
            kept[t] = send(kept[t], left_to_left(2 * t), mate_to_owner(t))
    return place_blocks(role, half, sent, kept)


def on_device(dosages, allele_counts, partner):
    cohorts, blocks = lax.axis_size("cohort"), lax.axis_size("person")
    rounds = [
        functools.partial(one_round, round_number, cohorts, blocks)
        for round_number in range(1, cohorts)
    ]
    own = load_rows(dosages[0])
    return lax.switch(partner[0] - 1, rounds, own, allele_counts[0])


def solution(mesh):
    placed = (P("cohort", "person", None), P("cohort", "person", None), P())
    return jax.shard_map(
        on_device,
        mesh=mesh,
        in_specs=placed,
        out_specs=P("cohort", "person", None),
        check_vma=False,
    )
```

time: 45.7 us -> 40.1 us (0.88)
  blocking collectives: 0 us -> 10.3 us
  starting transfers between devices: 29.1 us -> 19.6 us
  waiting for transfers between devices: 12.3 us -> 4.77 us
  local copies, waits for them, and re-layouts: 2.06 us -> 2.86 us
    all_to_all x0 -> x1, blocking collectives: none -> 10.3 us  [one_round(): totals = sum_of(lax.all_to_all(spread, 'person', 0, 0, tiled=True))]
    ppermute x12 -> x11, starting transfers between devices: 25.3 us -> 19.6 us  [send(): return lax.ppermute(value, AXES, pairs)]
    ppermute x12 -> x11, waiting for transfers between devices: 10 us -> 4.77 us  [send(): return lax.ppermute(value, AXES, pairs)]
    ppermute x4 -> x0, starting transfers between devices: 3.8 us -> none  [the longest x3 3.68 us: on_device(): lax.ppermute(counts, 'person', [(i, i ^ step) for i in range(blocks)])]
    ppermute x4 -> x0, waiting for transfers between devices: 2.26 us -> none  [the longest x3 2.25 us: on_device(): lax.ppermute(counts, 'person', [(i, i ^ step) for i in range(blocks)])]
    unnamed x8, local copies, waits for them, and re-layouts: 2.06 us -> 2.83 us
  transfers between devices with their start and end apart: 16 -> 11, of which waited for: 9 -> 3; matrix products, arithmetic and copies ran while one was open for 0% -> 0% of each run, Pallas kernels for 0% -> 0%
where the time goes in v6:
time: 40.1 us; the launch traced here: 39.8 us
  starting transfers between devices  19.6 us (49%)
  blocking collectives  10.3 us (26%)
  waiting for transfers between devices  4.77 us (12%)
  local copies, waits for them, and re-layouts  2.86 us (7%)
  Pallas kernels  2 us (5%)
    ppermute x11, starting transfers between devices, send(): return lax.ppermute(value, AXES, pairs)  19.6 us
    all_to_all x1, blocking collectives, one_round(): totals = sum_of(lax.all_to_all(spread, 'person', 0, 0, tiled=True))  10.3 us
    ppermute x11, waiting for transfers between devices, send(): return lax.ppermute(value, AXES, pairs)  4.77 us
    unnamed x8, local copies, waits for them, and re-layouts  2.83 us
    pallas_call x1, Pallas kernels, multiply(): pl.pallas_call(functools.partial(multiply_kernel, half, people_all), out_...  1.19 us
  transfers between devices with their start and end apart: 11, of which 3 were waited for; matrix products, arithmetic and copies ran while one was open for 0% of the time, Pallas kernels for 0%

profile of v6, /device:TPU:1, one launch (start us, length us, event | category | flops | bytes accessed | tf_op | source)
XLA Modules:
  0.0 39.8 jit_solution(18366418100132323495)
XLA Ops:
  0.0 0.0 copy-start.3
  0.0 0.7 %copy-done.3 = s32[4]{0:T(128)S(1)} copy-done((s32[4]{0:T(128)S(1)}, s32[4]{0:T(128)}, u32[]{:S(2)}) %copy-start.3) | copy-done | bytes 40
  0.7 0.0 copy-start
  0.7 1.0 %copy-done = bf16[1,128,1536]{2,1,0:T(8,128)(2,1)S(1)} copy-done((bf16[1,128,1536]{2,1,0:T(8,128)(2,1)S(1)}, bf16[1,128,1536]{2,1,0:T(8,128)(2,1)}, u32[]{:S(2)}) %copy-start) | copy-done | bytes 393240
  1.7 0.0 copy-start.2
  1.7 0.2 shard_map.43
  1.9 0.5 %copy-done.2 = s32[1,1,1536]{2,1,0:T(1,128)S(1)} copy-done((s32[1,1,1536]{2,1,0:T(1,128)S(1)}, s32[1,1,1536]{2,1,0:T(1,128)}, u32[]{:S(2)}) %copy-start.2) | copy-done | bytes 6168
  2.4 36.7 %conditional.1 = (bf16[1,128,1024]{2,1,0:T(8,128)(2,1)S(1)}) conditional(s32[]{:T(128)} %bitcast.9, (bf16[128,1536]{1,0:T(8,128)(2,1)S(1)}, s32[1,1,1536]{2,1,0:T(1,128)S(1)}) %tuple.28, (bf16[128,1536]{1,0:T(8,128)(2,1)S(1)}, s32[1,1,1536]{2,1,0:T(1,128)S(1)}) %tuple.29, (bf16[128,1536]{1,0:T(8,128)(2,1)S(1)}, ...), branch_computations={%region_0.0_spmd, %region_1.0_spmd, %region_2.0_spmd} | conditional | flops 11 | bytes 9128482 | solution.py:235
  2.4 0.1 collective-permute-start.10
  2.4 4.6 %collective-permute-start.9 = (bf16[128,1536]{1,0:T(8,128)(2,1)S(1)}, bf16[128,1536]{1,0:T(8,128)(2,1)S(1)}, u32[]{:S(2)}, u32[]{:S(2)}) collective-permute-start(bf16[128,1536]{1,0:T(8,128)(2,1)S(1)} %get-tuple-element.30.refs_0_), channel_id=1, source_target_pairs={{0,2},{8,20},{1,3},{9,21},{2,0},{10,22},{3,1},{11,23},{4,6},{12,16... | collective-permute-start | bytes 1179656 | tf_op jit(solution)/shard_map/cond/branch_1_fun/ppermute | solution.py:167
  7.0 0.0 collective-permute-done.10
  7.0 1.2 %collective-permute-start.11 = (bf16[128,1536]{1,0:T(8,128)(2,1)S(1)}, bf16[128,1536]{1,0:T(8,128)(2,1)S(1)}, u32[]{:S(2)}, u32[]{:S(2)}) collective-permute-start(bf16[128,1536]{1,0:T(8,128)(2,1)S(1)} %collective-permute-done.10), channel_id=1, source_target_pairs={{0,24},{8,9},{1,25},{9,8},{2,26},{10,11},{3,27},{11,10},{4,28},{12... | collective-permute-start | bytes 1179656 | tf_op jit(solution)/shard_map/cond/branch_1_fun/ppermute | solution.py:167
  8.3 10.3 %all_to_all.13.parts_ref = s32[8,1,1536]{2,1,0:T(1,128)S(1)} all-to-all(s32[8,1,1536]{2,1,0:T(1,128)S(1)} %broadcast_in_dim.17), channel_id=1, replica_groups=mesh['cohort'=4,'person'=8] {'person'}, dimensions={0} | all-to-all | bytes 98304 | tf_op jit(solution)/shard_map/cond/branch_1_fun/all_to_all | solution.py:210
  18.6 0.0 collective-permute-done.9.refs_1_
  18.7 1.0 %collective-permute-start.12 = (bf16[128,1536]{1,0:T(8,128)(2,1)S(1)}, bf16[128,1536]{1,0:T(8,128)(2,1)S(1)}, u32[]{:S(2)}, u32[]{:S(2)}) collective-permute-start(bf16[128,1536]{1,0:T(8,128)(2,1)S(1)} %collective-permute-done.9.refs_1_), channel_id=1, source_target_pairs={{0,9},{8,0},{1,8},{9,1},{2,11},{10,2},{3,10},{11,3},{4,13},{12,4},... | collective-permute-start | bytes 1179656 | tf_op jit(solution)/shard_map/cond/branch_1_fun/ppermute | solution.py:167
  19.7 0.0 collective-permute-done.11.refs_2_
  19.7 0.1 collective-permute-start.13
  19.8 0.7 %collective-permute-start.15 = (s32[1,1536]{1,0:T(1,128)S(1)}, s32[1,1536]{1,0:T(1,128)S(1)}, u32[]{:S(2)}, u32[]{:S(2)}) collective-permute-start(s32[1,1536]{1,0:T(1,128)S(1)} %branch_1_fun.3), channel_id=1, source_target_pairs={{0,8},{16,0},{1,9},{17,1},{2,10},{18,2},{3,11},{19,3},{4,12},{20,4... | collective-permute-start | bytes 18440 | tf_op jit(solution)/shard_map/cond/branch_1_fun/ppermute | solution.py:167
  20.5 3.2 %collective-permute-start.14 = (s32[1,1536]{1,0:T(1,128)S(1)}, s32[1,1536]{1,0:T(1,128)S(1)}, u32[]{:S(2)}, u32[]{:S(2)}) collective-permute-start(s32[1,1536]{1,0:T(1,128)S(1)} %branch_1_fun.3), channel_id=1, source_target_pairs={{0,0},{16,8},{1,1},{17,9},{2,2},{18,10},{3,3},{19,11},{4,4},{20,12... | collective-permute-start | bytes 18440 | tf_op jit(solution)/shard_map/cond/branch_1_fun/ppermute | solution.py:167
  23.7 0.1 pad_add_fusion.1.role_ref
  23.8 0.0 collective-permute-done.15.refs_7_
  23.8 1.6 %collective-permute-done.14.refs_6_ = s32[1,1536]{1,0:T(1,128)S(1)} collective-permute-done((s32[1,1536]{1,0:T(1,128)S(1)}, s32[1,1536]{1,0:T(1,128)S(1)}, u32[]{:S(2)}, u32[]{:S(2)}) %collective-permute-start.14) | collective-permute-done | bytes 6176 | tf_op jit(solution)/shard_map/cond/branch_1_fun/ppermute | solution.py:167
  25.4 0.5 %collective-permute-done.12.refs_3_.refs_5_ = bf16[128,1536]{1,0:T(8,128)(2,1)S(1)} collective-permute-done((bf16[128,1536]{1,0:T(8,128)(2,1)S(1)}, bf16[128,1536]{1,0:T(8,128)(2,1)S(1)}, u32[]{:S(2)}, u32[]{:S(2)}) %collective-permute-start.12) | collective-permute-done | bytes 393248 | tf_op jit(solution)/shard_map/cond/branch_1_fun/ppermute | solution.py:167
  25.9 0.0 collective-permute-done.13.refs_4_
  25.9 1.2 %branch_1_fun.4 = (bf16[128,256]{1,0:T(8,128)(2,1)S(1)}, bf16[128,256]{1,0:T(8,128)(2,1)S(1)}, bf16[128,256]{1,0:T(8,128)(2,1)S(1)}, bf16[128,256]{1,0:T(8,128)(2,1)S(1)}) custom-call(s32[2]{0:T(128)S(1)} %pad_add_fusion.1.role_ref, bf16[128,1536]{1,0:T(8,128)(2,1)S(1)} %get-tuple-element.30.refs_0_, bf16[128,1536]{1,0:T(8,128)(2,1)S(1)} %collective-permute-done.9.refs_1_, ...), custom_call_target="tpu_custom_call" | custom-call | tf_op jit(solution)/shard_map/cond/branch_1_fun/pallas_call | solution.py:108
  27.1 0.1 collective-permute-start.16
  27.2 2.2 %collective-permute-start.17 = (bf16[128,256]{1,0:T(8,128)(2,1)S(1)}, bf16[128,256]{1,0:T(8,128)(2,1)S(1)}, u32[]{:S(2)}, u32[]{:S(2)}) collective-permute-start(bf16[128,256]{1,0:T(8,128)(2,1)S(1)} %get-tuple-element.36), channel_id=1, source_target_pairs={{8,3},{0,20},{9,2},{1,21},{10,1},{2,22},{11,0},{3,23},{12,7},{4,16... | collective-permute-start | bytes 196616 | tf_op jit(solution)/shard_map/cond/branch_1_fun/ppermute | solution.py:167
  29.4 2.1 %collective-permute-start.18 = (bf16[128,256]{1,0:T(8,128)(2,1)S(1)}, bf16[128,256]{1,0:T(8,128)(2,1)S(1)}, u32[]{:S(2)}, u32[]{:S(2)}) collective-permute-start(bf16[128,256]{1,0:T(8,128)(2,1)S(1)} %get-tuple-element.37), channel_id=1, source_target_pairs={{0,0},{8,16},{1,1},{9,17},{2,2},{10,18},{3,3},{11,19},{4,4},{12,20... | collective-permute-start | bytes 196616 | tf_op jit(solution)/shard_map/cond/branch_1_fun/ppermute | solution.py:167
  31.5 4.3 %collective-permute-start.19 = (bf16[128,256]{1,0:T(8,128)(2,1)S(1)}, bf16[128,256]{1,0:T(8,128)(2,1)S(1)}, u32[]{:S(2)}, u32[]{:S(2)}) collective-permute-start(bf16[128,256]{1,0:T(8,128)(2,1)S(1)} %get-tuple-element.38), channel_id=1, source_target_pairs={{0,2},{8,20},{1,3},{9,21},{2,0},{10,22},{3,1},{11,23},{4,6},{12,16... | collective-permute-start | bytes 196616 | tf_op jit(solution)/shard_map/cond/branch_1_fun/ppermute | solution.py:167
  35.8 0.0 collective-permute-done.16.refs_0_
  35.8 0.0 collective-permute-done.17.refs_1_
  35.8 0.0 collective-permute-done.18.refs_2_
  35.8 2.6 %collective-permute-done.19.refs_3_ = bf16[128,256]{1,0:T(8,128)(2,1)S(1)} collective-permute-done((bf16[128,256]{1,0:T(8,128)(2,1)S(1)}, bf16[128,256]{1,0:T(8,128)(2,1)S(1)}, u32[]{:S(2)}, u32[]{:S(2)}) %collective-permute-start.19) | collective-permute-done | bytes 65568 | tf_op jit(solution)/shard_map/cond/branch_1_fun/ppermute | solution.py:167
  38.5 0.6 %branch_1_fun.5 = bf16[1,128,1024]{2,1,0:T(8,128)(2,1)S(1)} custom-call(s32[2]{0:T(128)S(1)} %pad_add_fusion.1.role_ref, bf16[128,256]{1,0:T(8,128)(2,1)S(1)} %collective-permute-done.16.refs_0_, bf16[128,256]{1,0:T(8,128)(2,1)S(1)} %collective-permute-done.17.refs_1_, bf16[128,256]{1,0:T(8,128)(2,1)S(1)} %collective-permute-done.18.refs_2_, ...), custom_call_target="tpu_custom_call" | custom-call | tf_op jit(solution)/shard_map/cond/branch_1_fun/pallas_call | solution.py:146
  39.1 0.0 copy-start.1
  39.1 0.7 %copy-done.1 = bf16[1,128,1024]{2,1,0:T(8,128)(2,1)} copy-done((bf16[1,128,1024]{2,1,0:T(8,128)(2,1)}, bf16[1,128,1024]{2,1,0:T(8,128)(2,1)S(1)}, u32[]{:S(2)}) %copy-start.1) | copy-done | bytes 262168
  (3 shorter events, 0.1 us)
Async XLA Ops:
  0.0 0.7 %copy-start.3 = (s32[4]{0:T(128)S(1)}, s32[4]{0:T(128)}, u32[]{:S(2)}) copy-start(s32[4]{0:T(128)} %param.8) | copy-start | bytes 52
  0.7 1.0 %copy-start = (bf16[1,128,1536]{2,1,0:T(8,128)(2,1)S(1)}, bf16[1,128,1536]{2,1,0:T(8,128)(2,1)}, u32[]{:S(2)}) copy-start(bf16[1,128,1536]{2,1,0:T(8,128)(2,1)} %param.6) | copy-start | bytes 1179652
  1.7 0.7 %copy-start.2 = (s32[1,1,1536]{2,1,0:T(1,128)S(1)}, s32[1,1,1536]{2,1,0:T(1,128)}, u32[]{:S(2)}) copy-start(s32[1,1,1536]{2,1,0:T(1,128)} %param.7) | copy-start | bytes 18436
  2.4 4.6 %collective-permute-start.10 = (bf16[128,1536]{1,0:T(8,128)(2,1)S(1)}, bf16[128,1536]{1,0:T(8,128)(2,1)S(1)}, u32[]{:S(2)}, u32[]{:S(2)}) collective-permute-start(bf16[128,1536]{1,0:T(8,128)(2,1)S(1)} %get-tuple-element.30.refs_0_), channel_id=1, source_target_pairs={{0,8},{8,0},{1,9},{9,1},{2,10},{10,2},{3,11},{11,3},{4,12},{12,4},... | collective-permute-start | bytes 1179656 | tf_op jit(solution)/shard_map/cond/branch_1_fun/ppermute | solution.py:167
  2.4 16.2 %collective-permute-start.9 = (bf16[128,1536]{1,0:T(8,128)(2,1)S(1)}, bf16[128,1536]{1,0:T(8,128)(2,1)S(1)}, u32[]{:S(2)}, u32[]{:S(2)}) collective-permute-start(bf16[128,1536]{1,0:T(8,128)(2,1)S(1)} %get-tuple-element.30.refs_0_), channel_id=1, source_target_pairs={{0,2},{8,20},{1,3},{9,21},{2,0},{10,22},{3,1},{11,23},{4,6},{12,16... | collective-permute-start | bytes 1179656 | tf_op jit(solution)/shard_map/cond/branch_1_fun/ppermute | solution.py:167
  7.0 12.6 %collective-permute-start.11 = (bf16[128,1536]{1,0:T(8,128)(2,1)S(1)}, bf16[128,1536]{1,0:T(8,128)(2,1)S(1)}, u32[]{:S(2)}, u32[]{:S(2)}) collective-permute-start(bf16[128,1536]{1,0:T(8,128)(2,1)S(1)} %collective-permute-done.10), channel_id=1, source_target_pairs={{0,24},{8,9},{1,25},{9,8},{2,26},{10,11},{3,27},{11,10},{4,28},{12... | collective-permute-start | bytes 1179656 | tf_op jit(solution)/shard_map/cond/branch_1_fun/ppermute | solution.py:167
  18.7 7.3 %collective-permute-start.12 = (bf16[128,1536]{1,0:T(8,128)(2,1)S(1)}, bf16[128,1536]{1,0:T(8,128)(2,1)S(1)}, u32[]{:S(2)}, u32[]{:S(2)}) collective-permute-start(bf16[128,1536]{1,0:T(8,128)(2,1)S(1)} %collective-permute-done.9.refs_1_), channel_id=1, source_target_pairs={{0,9},{8,0},{1,8},{9,1},{2,11},{10,2},{3,10},{11,3},{4,13},{12,4},... | collective-permute-start | bytes 1179656 | tf_op jit(solution)/shard_map/cond/branch_1_fun/ppermute | solution.py:167
  19.7 6.2 %collective-permute-start.13 = (bf16[128,1536]{1,0:T(8,128)(2,1)S(1)}, bf16[128,1536]{1,0:T(8,128)(2,1)S(1)}, u32[]{:S(2)}, u32[]{:S(2)}) collective-permute-start(bf16[128,1536]{1,0:T(8,128)(2,1)S(1)} %collective-permute-done.11.refs_2_), channel_id=1, source_target_pairs={{0,8},{8,0},{1,9},{9,1},{2,10},{10,2},{3,11},{11,3},{4,12},{12,4},... | collective-permute-start | bytes 1179656 | tf_op jit(solution)/shard_map/cond/branch_1_fun/ppermute | solution.py:167
  19.8 4.0 %collective-permute-start.15 = (s32[1,1536]{1,0:T(1,128)S(1)}, s32[1,1536]{1,0:T(1,128)S(1)}, u32[]{:S(2)}, u32[]{:S(2)}) collective-permute-start(s32[1,1536]{1,0:T(1,128)S(1)} %branch_1_fun.3), channel_id=1, source_target_pairs={{0,8},{16,0},{1,9},{17,1},{2,10},{18,2},{3,11},{19,3},{4,12},{20,4... | collective-permute-start | bytes 18440 | tf_op jit(solution)/shard_map/cond/branch_1_fun/ppermute | solution.py:167
  20.5 4.9 %collective-permute-start.14 = (s32[1,1536]{1,0:T(1,128)S(1)}, s32[1,1536]{1,0:T(1,128)S(1)}, u32[]{:S(2)}, u32[]{:S(2)}) collective-permute-start(s32[1,1536]{1,0:T(1,128)S(1)} %branch_1_fun.3), channel_id=1, source_target_pairs={{0,0},{16,8},{1,1},{17,9},{2,2},{18,10},{3,3},{19,11},{4,4},{20,12... | collective-permute-start | bytes 18440 | tf_op jit(solution)/shard_map/cond/branch_1_fun/ppermute | solution.py:167
  27.1 8.7 %collective-permute-start.16 = (bf16[128,256]{1,0:T(8,128)(2,1)S(1)}, bf16[128,256]{1,0:T(8,128)(2,1)S(1)}, u32[]{:S(2)}, u32[]{:S(2)}) collective-permute-start(bf16[128,256]{1,0:T(8,128)(2,1)S(1)} %get-tuple-element.35), channel_id=1, source_target_pairs={{8,1},{0,16},{9,0},{1,17},{10,3},{2,18},{11,2},{3,19},{12,5},{4,20... | collective-permute-start | bytes 196616 | tf_op jit(solution)/shard_map/cond/branch_1_fun/ppermute | solution.py:167
  27.2 8.6 %collective-permute-start.17 = (bf16[128,256]{1,0:T(8,128)(2,1)S(1)}, bf16[128,256]{1,0:T(8,128)(2,1)S(1)}, u32[]{:S(2)}, u32[]{:S(2)}) collective-permute-start(bf16[128,256]{1,0:T(8,128)(2,1)S(1)} %get-tuple-element.36), channel_id=1, source_target_pairs={{8,3},{0,20},{9,2},{1,21},{10,1},{2,22},{11,0},{3,23},{12,7},{4,16... | collective-permute-start | bytes 196616 | tf_op jit(solution)/shard_map/cond/branch_1_fun/ppermute | solution.py:167
  29.4 6.4 %collective-permute-start.18 = (bf16[128,256]{1,0:T(8,128)(2,1)S(1)}, bf16[128,256]{1,0:T(8,128)(2,1)S(1)}, u32[]{:S(2)}, u32[]{:S(2)}) collective-permute-start(bf16[128,256]{1,0:T(8,128)(2,1)S(1)} %get-tuple-element.37), channel_id=1, source_target_pairs={{0,0},{8,16},{1,1},{9,17},{2,2},{10,18},{3,3},{11,19},{4,4},{12,20... | collective-permute-start | bytes 196616 | tf_op jit(solution)/shard_map/cond/branch_1_fun/ppermute | solution.py:167
  31.5 6.9 %collective-permute-start.19 = (bf16[128,256]{1,0:T(8,128)(2,1)S(1)}, bf16[128,256]{1,0:T(8,128)(2,1)S(1)}, u32[]{:S(2)}, u32[]{:S(2)}) collective-permute-start(bf16[128,256]{1,0:T(8,128)(2,1)S(1)} %get-tuple-element.38), channel_id=1, source_target_pairs={{0,2},{8,20},{1,3},{9,21},{2,0},{10,22},{3,1},{11,23},{4,6},{12,16... | collective-permute-start | bytes 196616 | tf_op jit(solution)/shard_map/cond/branch_1_fun/ppermute | solution.py:167
  39.1 0.7 %copy-start.1 = (bf16[1,128,1024]{2,1,0:T(8,128)(2,1)}, bf16[1,128,1024]{2,1,0:T(8,128)(2,1)S(1)}, u32[]{:S(2)}) copy-start(bf16[1,128,1024]{2,1,0:T(8,128)(2,1)S(1)} %get-tuple-element.117) | copy-start | bytes 786436
